TPU v7x, 32 devices: a whole 2x2x4 slice. The times are simulated.
32 devices in a mesh: groups: 2 (over x), ctx: 4 (over y, core), chan: 4 (over z).
Axes of the slice: x: 2, y: 2, z: 4, core: 2. Of those that a mesh axis runs over, the one named last changes fastest.
Arguments:
- stretch_rows: bfloat16 [96, 16, 3, 8192], P(('groups', 'ctx'), None, None, 'chan'), parts along dimension 0, may hold values from -6 to 6
- stretch_owner: int32 [96], P(('groups', 'ctx')), parts along dimension 0, may hold values from 0 to 3, as said below
- send_slot: int32 [8, 4, 6], P(('groups', 'ctx')), parts along dimension 0, may hold values from -1 to 15, as said below
- decode_rows: bfloat16 [128, 3, 8192], P(('groups', 'ctx'), None, 'chan'), parts along dimension 0, may hold values from -6 to 6
- row_owner: int32 [128], P(('groups', 'ctx')), parts along dimension 0, may hold values from 0 to 3, as said below
- row_slot: int32 [128], P(('groups', 'ctx')), parts along dimension 0, may hold values from 0 to 15
- cache_raw: bfloat16 [128, 6, 3, 8192], P(('groups', 'ctx'), None, None, 'chan'), parts along dimension 0, may hold values from -6 to 6
- cache_hist: bfloat16 [128, 127, 8192], P(('groups', 'ctx'), None, 'chan'), parts along dimension 0, may hold values from -6 to 6
- short_weight: bfloat16 [7, 3, 8192], P(None, None, 'chan'), may hold values from -2 to 2
- long_filter: bfloat16 [512, 128], P('chan'), may hold values from -0.5 to 0.5
Outputs:
- stretch_out: bfloat16 [96, 16, 8192], P(('groups', 'ctx'), None, 'chan'), parts along dimension 0
- decode_out: bfloat16 [128, 8192], P(('groups', 'ctx'), 'chan'), parts along dimension 0
There are 2 independent parts, one for each index of `groups`. A program takes and returns all parts, laid end to end along the dimension named above; an argument that names none is the same for every part. Nothing has to cross between parts.
Inputs may be any that keep to these rules, and one draw needn't show every extreme that they name: `stretch_owner`: among the stretches of one ctx index at most 6 name the same owner; one owner, drawn from the seed, is named by exactly 6 stretches of every ctx index. send_slot[o, d, r] is the cache slot on owner o of the stretch of ctx index d that is the r-th (in stretch order, from 0) of that index to name owner o, and -1 where ctx index d has r or fewer such stretches. `row_owner`: among the decode rows of one ctx index at most 8 name the same owner; one owner, drawn from the seed, is named by exactly 8 rows of every ctx index.
All inputs are finite; a program needn't handle non-finite values.
Results may differ from a plain program's by a relative error of at most 0.0035.
Values may be sent and summed in bfloat16 or wider, within the bound.
No kernel may reach another device: no remote copies, remote signals or barrier semaphores. Data moves between devices by JAX's collectives and lax.ppermute only.
A program may use at most 128 MiB of HBM per device.

v0:
```python
import jax
import jax.numpy as jnp
from jax import lax
from jax.sharding import PartitionSpec as P


def short_part(stretch_block, raw_state, short_weight):
    length = stretch_block.shape[1]
    taps_short = short_weight.shape[0]
    extended = jnp.concatenate([raw_state, stretch_block], axis=1)
    featured = jnp.zeros(stretch_block.shape, jnp.float32)
    for tap_index in range(taps_short):
        offset_tap = taps_short - 1 - tap_index
        window = extended[:, offset_tap : offset_tap + length].astype(jnp.float32)
        featured = featured + short_weight[tap_index].astype(jnp.float32) * window
    return featured


def toeplitz_of(long_filter, length, span_width, shift):
    taps_long = long_filter.shape[1]
    lag_table = jnp.arange(length)[:, None] + shift - jnp.arange(span_width)[None, :]
    in_band = (lag_table >= 0) & (lag_table < taps_long)
    tap_values = jnp.take(long_filter, jnp.clip(lag_table, 0, taps_long - 1), axis=1)
    return jnp.where(in_band[None], tap_values, jnp.zeros_like(tap_values))


def grouped_conv(toeplitz, history):
    group_count = toeplitz.shape[0]
    row_count, span_width, channels = history.shape
    length = toeplitz.shape[1]
    per_group = channels // group_count
    arranged = history.reshape(row_count, span_width, group_count, per_group)
    arranged = arranged.transpose(2, 1, 0, 3).reshape(
        group_count, span_width, row_count * per_group
    )
    convolved = jnp.einsum("gim,gmx->gix", toeplitz, arranged, preferred_element_type=jnp.float32)
    convolved = convolved.reshape(group_count, length, row_count, per_group).transpose(2, 1, 0, 3)
    return convolved.reshape(row_count, length, channels)


def featurize(stretch_block, raw_state, hist_state, short_weight, long_filter):
    length = stretch_block.shape[1]
    taps_long = long_filter.shape[1]
    featured = short_part(stretch_block, raw_state, short_weight)
    product = (featured[:, :, 1] * featured[:, :, 2]).astype(jnp.bfloat16)
    history = jnp.concatenate([hist_state, product], axis=1)
    toeplitz = toeplitz_of(long_filter, length, history.shape[1], taps_long - 1)
    convolved = grouped_conv(toeplitz, history)
    return (featured[:, :, 0] * convolved).astype(jnp.bfloat16)


def bucket_of(owners, capacity):
    row_count = owners.shape[0]
    same_owner = owners[:, None] == owners[None, :]
    earlier = jnp.arange(row_count)[None, :] < jnp.arange(row_count)[:, None]
    owner_rank = jnp.sum(same_owner & earlier, axis=1)
    return owners * capacity + owner_rank


def per_device(
    stretch_rows,
    stretch_owner,
    send_slot,
    decode_rows,
    row_owner,
    row_slot,
    cache_raw,
    cache_hist,
    short_weight,
    long_filter,
):
    peer_count = lax.axis_size("ctx")
    stretch_cap = send_slot.shape[2]
    channels = stretch_rows.shape[-1]
    raw_rows = cache_raw.shape[1]
    hist_rows = cache_hist.shape[1]
    bucket = bucket_of(stretch_owner, stretch_cap)
    safe_slots = jnp.maximum(send_slot[0], 0).reshape(-1)
    out_raw = jnp.take(cache_raw, safe_slots, axis=0).reshape(
        peer_count, stretch_cap, raw_rows, 3, channels
    )
    out_hist = jnp.take(cache_hist, safe_slots, axis=0).reshape(
        peer_count, stretch_cap, hist_rows, channels
    )
    got_raw, got_hist = (
        lax.all_to_all(out_raw, "ctx", split_axis=0, concat_axis=0, tiled=True),
        lax.all_to_all(out_hist, "ctx", split_axis=0, concat_axis=0, tiled=True),
    )
    raw_state = jnp.take(
        got_raw.reshape(peer_count * stretch_cap, raw_rows, 3, channels), bucket, axis=0
    )
    hist_state = jnp.take(
        got_hist.reshape(peer_count * stretch_cap, hist_rows, channels), bucket, axis=0
    )
    stretch_out = featurize(stretch_rows, raw_state, hist_state, short_weight, long_filter)
    decode_count = decode_rows.shape[0]
    decode_cap = max(2, (2 * decode_count + peer_count - 1) // peer_count)
    decode_bucket = bucket_of(row_owner, decode_cap)
    send_rows = jnp.zeros((peer_count * decode_cap, 3, channels), jnp.bfloat16)
    send_rows = (
        send_rows.at[decode_bucket].set(decode_rows).reshape(peer_count, decode_cap, 3, channels)
    )
    send_ids = jnp.full((peer_count * decode_cap,), -1, jnp.int32)
    send_ids = send_ids.at[decode_bucket].set(row_slot).reshape(peer_count, decode_cap)
    arrived_rows = lax.all_to_all(send_rows, "ctx", split_axis=0, concat_axis=0, tiled=True)
    arrived_ids = lax.all_to_all(send_ids, "ctx", split_axis=0, concat_axis=0, tiled=True)
    per_source = arrived_ids.shape[1]
    flat_ids = jnp.maximum(arrived_ids, 0).reshape(-1)
    raw_state = jnp.take(cache_raw, flat_ids, axis=0)
    hist_state = jnp.take(cache_hist, flat_ids, axis=0)
    single = arrived_rows.reshape(peer_count * per_source, 1, 3, channels)
    results = featurize(single, raw_state, hist_state, short_weight, long_filter)
    returned_rows = lax.all_to_all(
        results.reshape(peer_count, per_source, channels),
        "ctx",
        split_axis=0,
        concat_axis=0,
        tiled=True,
    )
    decode_out = jnp.take(
        returned_rows.reshape(peer_count * decode_cap, channels), decode_bucket, axis=0
    )
    return (stretch_out, decode_out)


def solution(mesh):
    placed = (
        P(("groups", "ctx"), None, None, "chan"),
        P(("groups", "ctx")),
        P(("groups", "ctx"), None, None),
        P(("groups", "ctx"), None, "chan"),
        P(("groups", "ctx")),
        P(("groups", "ctx")),
        P(("groups", "ctx"), None, None, "chan"),
        P(("groups", "ctx"), None, "chan"),
        P(None, None, "chan"),
        P("chan", None),
    )
    return jax.shard_map(
        per_device,
        mesh=mesh,
        in_specs=placed,
        out_specs=(P(("groups", "ctx"), None, "chan"), P(("groups", "ctx"), "chan")),
        check_vma=False,
    )
```

profile of v0, /device:TPU:0, one launch (start us, length us, event | category | flops | bytes accessed | tf_op | source)
XLA Modules:
  0.0 454.4 jit_solution(6680058064514427601)
XLA Ops:
  11.5 6.4 %gather_fusion = bf16[24,6,3,2048]{3,0,2,1:T(8,128)(2,1)S(1)} fusion(bf16[16,6,3,2048]{3,0,2,1:T(8,128)(2,1)S(1)} %copy-done, s32[1024]{0:T(1024)S(1)} %pad_clamp_fusion.5), kind=kCustom, calls=%fused_computation | custom fusion | bytes 3539040 | tf_op jit(solution)/shard_map/jit(_take)/gather | solution.py:79
  31.3 8.7 %gather_fusion.5 = bf16[32,6,3,2048]{3,0,2,1:T(8,128)(2,1)} fusion(bf16[16,6,3,2048]{3,0,2,1:T(8,128)(2,1)S(1)} %copy-done, s32[1024]{0:T(1024)S(1)} %pad_clamp_fusion.3), kind=kCustom, calls=%fused_computation.5 | custom fusion | bytes 4718720 | tf_op jit(solution)/shard_map/jit(_take)/gather | solution.py:109
  40.2 31.9 %gather_fusion.7 = bf16[32,127,2048]{2,0,1:T(8,128)(2,1)} fusion(bf16[16,127,2048]{2,0,1:T(8,128)(2,1)} %param.17, s32[1024]{0:T(1024)S(1)} %pad_clamp_fusion.3), kind=kCustom, calls=%fused_computation.7 | custom fusion | bytes 33292416 | tf_op jit(solution)/shard_map/jit(_take)/gather | solution.py:110
  72.0 24.1 %copy.110 = bf16[32,127,2048]{1,2,0:T(8,128)(2,1)} copy(bf16[32,127,2048]{2,0,1:T(8,128)(2,1)} %gather_fusion.7) | data formatting | bytes 33292288 | tf_op jit(solution)/shard_map/jit(_take)/gather | solution.py:110
  96.2 14.3 %broadcast_select_fusion = bf16[32,127,128,16]{1,3,2,0:T(8,128)(2,1)} fusion(bf16[32,127,128,16]{1,3,2,0:T(8,128)(2,1)} %bitcast.86, pred[32]{0:T(512)(128)(4,1)S(1)} %le.69), kind=kLoop, calls=%fused_computation.13 | loop fusion | flops 8323072 | bytes 33292320 | tf_op jit(solution)/shard_map/jit(_take)/select_n | solution.py:110
  113.2 16.9 %copy.112 = bf16[32,1,128,16]{1,3,2,0:T(8,128)(2,1)} copy(bf16[32,1,128,16]{0,3,2,1:T(8,128)(2,1)S(1)} %bitcast.97) | data formatting | bytes 262144 | tf_op jit(solution)/shard_map/convert_element_type | solution.py:45
  130.1 15.3 %maximum_bitcast_fusion = bf16[128,128,32,16]{1,3,0,2:T(8,128)(2,1)S(1)} fusion(bf16[32,1,128,16]{1,3,2,0:T(8,128)(2,1)} %copy.112, bf16[32,127,128,16]{1,3,2,0:T(8,128)(2,1)} %broadcast_select_fusion), kind=kLoop, calls=%fused_computation.12 | loop fusion | flops 33554432 | bytes 33554432 | tf_op jit(solution)/shard_map/transpose | solution.py:33
  147.4 9.5 %multiply_reduce_fusion = f32[128,512]{1,0:T(8,128)S(1)} fusion(bf16[128,128,512]{1,2,0:T(8,128)(2,1)S(1)} %bitcast.85, f32[128,128]{1,0:T(8,128)S(1)} %copy-done.23), kind=kLoop, calls=%fused_computation.11 | loop fusion | flops 25100288 | bytes 17104896
  176.5 25.7 %gather_fusion.3 = bf16[24,127,2048]{2,0,1:T(8,128)(2,1)} fusion(bf16[16,127,2048]{2,0,1:T(8,128)(2,1)} %param.17, s32[1024]{0:T(1024)S(1)} %pad_clamp_fusion.5), kind=kCustom, calls=%fused_computation.3 | custom fusion | bytes 24969312 | tf_op jit(solution)/shard_map/jit(_take)/gather | solution.py:82
  202.2 11.9 %copy.97 = bf16[24,127,2048]{2,1,0:T(8,128)(2,1)S(1)} copy(bf16[24,127,2048]{2,0,1:T(8,128)(2,1)} %gather_fusion.3) | data formatting | bytes 24969216 | tf_op jit(solution)/shard_map/jit(_take)/gather | solution.py:82
  214.1 5.6 %broadcast_select_fusion.1 = bf16[4,6,127,2048]{3,2,1,0:T(8,128)(2,1)} fusion(bf16[4,6,127,2048]{3,2,1,0:T(8,128)(2,1)S(1)} %bitcast.87, pred[4,6]{1,0:T(4,128)(4,1)S(1)} %compare_bitcast_fusion), kind=kLoop, calls=%fused_computation.15 | loop fusion | flops 6242304 | bytes 24969240 | tf_op jit(solution)/shard_map/jit(_take)/select_n | solution.py:82
  221.1 6.5 %all-to-all-start.1 = ((bf16[4,6,127,2048]{3,2,1,0:T(8,128)(2,1)}), bf16[4,6,127,2048]{3,2,1,0:T(8,128)(2,1)}, u32[]{:S(2)}, u32[]{:S(2)}) async-start(bf16[4,6,127,2048]{3,2,1,0:T(8,128)(2,1)} %broadcast_select_fusion.1), calls=%async_computation.1 | async-start | bytes 25165824 | tf_op jit(solution)/shard_map/all_to_all | solution.py:87
  228.4 4.9 %gather_fusion.2 = bf16[2288,128]{1,0:T(8,128)(2,1)S(1)} fusion(bf16[128,128]{0,1:T(8,128)(2,1)S(1)} %copy-done.3, s32[3072]{0:T(1024)S(1)} %pad_clamp_fusion), kind=kCustom, calls=%fused_computation.2 | custom fusion | bytes 1180608 | tf_op jit(solution)/shard_map/jit(_take)/gather | solution.py:23
  236.9 4.4 copy.119
  257.0 4.5 copy.121
  261.5 104.3 %all-to-all-done.1 = bf16[4,6,127,2048]{3,2,1,0:T(8,128)(2,1)} async-done(((bf16[4,6,127,2048]{3,2,1,0:T(8,128)(2,1)}), bf16[4,6,127,2048]{3,2,1,0:T(8,128)(2,1)}, u32[]{:S(2)}, u32[]{:S(2)}) %all-to-all-start.1) | async-done | bytes 12484640 | tf_op jit(solution)/shard_map/all_to_all | solution.py:87
  365.7 8.7 %gather_fusion.4 = bf16[12,127,2048]{2,1,0:T(8,128)(2,1)} fusion(bf16[24,127,2048]{2,1,0:T(8,128)(2,1)} %bitcast.5, s32[1024]{0:T(1024)S(1)} %pad_clamp_fusion.4), kind=kCustom, calls=%fused_computation.4 | custom fusion | bytes 12484656 | tf_op jit(solution)/shard_map/jit(_take)/gather | solution.py:92
  374.5 9.0 %copy.98 = bf16[12,127,2048]{1,2,0:T(8,128)(2,1)} copy(bf16[12,127,2048]{2,1,0:T(8,128)(2,1)} %gather_fusion.4) | data formatting | bytes 12484608 | tf_op jit(solution)/shard_map/jit(_take)/gather | solution.py:92
  387.5 7.9 %maximum_bitcast_fusion.1 = bf16[128,143,12,16]{1,3,0,2:T(8,128)(2,1)} fusion(bf16[12,16,128,16]{1,3,2,0:T(8,128)(2,1)S(1)} %bitcast.92, bf16[12,127,128,16]{1,3,2,0:T(8,128)(2,1)S(1)} %broadcast_select_fusion.2), kind=kLoop, calls=%fused_computation.14 | loop fusion | flops 14057472 | bytes 14057472 | tf_op jit(solution)/shard_map/transpose | solution.py:33
  395.4 16.7 %copy.100 = bf16[128,143,12,16]{0,3,2,1:T(8,128)(2,1)} copy(bf16[128,143,12,16]{1,3,0,2:T(8,128)(2,1)} %maximum_bitcast_fusion.1) | data formatting | bytes 14057472 | tf_op jit(solution)/shard_map/transpose | solution.py:33
  412.1 13.4 %copy.102 = bf16[128,143,192]{2,1,0:T(8,128)(2,1)} copy(bf16[128,143,192]{0,2,1:T(8,128)(2,1)} %bitcast.88) | data formatting | bytes 14057472 | tf_op jit(solution)/shard_map/reshape | solution.py:33
  425.5 5.0 %fusion.28 = f32[128,16,192]{2,1,0:T(8,128)S(1)} fusion(bf16[128,16,143]{2,1,0:T(8,128)(2,1)S(1)} %copy.101, bf16[128,143,192]{2,1,0:T(8,128)(2,1)} %copy.102), kind=kOutput, calls=%fused_computation.109 | convolution fusion | flops 112459776 | bytes 9187328 | tf_op jit(solution)/shard_map/gim,gmx->gix/dot_general | solution.py:36
  432.3 8.0 %copy.104 = f32[12,16,128,16]{3,2,1,0:T(8,128)} copy(f32[12,16,128,16]{2,3,0,1:T(8,128)} %bitcast.93) | data formatting | bytes 3145728 | tf_op jit(solution)/shard_map/transpose | solution.py:37
  440.4 11.1 %reshape.368 = f32[12,16,2048]{2,1,0:T(8,128)S(1)} reshape(f32[12,16,128,16]{3,2,1,0:T(8,128)} %copy.104) | data formatting | bytes 3145728 | tf_op jit(solution)/shard_map/reshape | solution.py:38
  (136 shorter events, 78.0 us)
Async XLA Ops:
  0.6 10.8 %copy-start = (bf16[16,6,3,2048]{3,0,2,1:T(8,128)(2,1)S(1)}, bf16[16,6,3,2048]{3,0,2,1:T(8,128)(2,1)}, u32[]{:S(2)}) copy-start(bf16[16,6,3,2048]{3,0,2,1:T(8,128)(2,1)} %param.16) | copy-start | bytes 3538948
  2.7 18.5 %copy-start.26 = (s32[16]{0:T(128)}, s32[16]{0:T(128)S(1)}, u32[]{:S(2)}) copy-start(s32[16]{0:T(128)S(1)} %get-tuple-element.3) | copy-start | bytes 196
  4.2 22.7 %all-to-all-start.3 = ((s32[4,1,8]{2,1,0:T(1,128)}), s32[4,1,8]{2,1,0:T(1,128)S(1)}, u32[]{:S(2)}, u32[]{:S(2)}) async-start(s32[4,1,8]{2,1,0:T(1,128)} %bitcast.14), calls=%async_computation.3 | async-start | bytes 4096 | tf_op jit(solution)/shard_map/all_to_all | solution.py:106
  11.4 9.3 %copy-start.25 = (bf16[128,128]{1,0:T(8,128)(2,1)S(1)}, bf16[128,128]{1,0:T(8,128)(2,1)}, u32[]{:S(2)}) copy-start(bf16[128,128]{1,0:T(8,128)(2,1)} %param.19) | copy-start | bytes 98308
  11.5 9.4 %copy-start.24 = (bf16[16,3,2048]{2,0,1:T(8,128)(2,1)S(1)}, bf16[16,3,2048]{2,0,1:T(8,128)(2,1)}, u32[]{:S(2)}) copy-start(bf16[16,3,2048]{2,0,1:T(8,128)(2,1)} %param.13) | copy-start | bytes 589828
  20.9 19.2 %copy-start.2 = (bf16[128,128]{0,1:T(8,128)(2,1)}, bf16[128,128]{0,1:T(8,128)(2,1)S(1)}, u32[]{:S(2)}) copy-start(bf16[128,128]{0,1:T(8,128)(2,1)S(1)} %copy.96) | copy-start | bytes 98308
  26.9 83.9 %all-to-all-start.2 = ((bf16[4,8,3,2048]{3,1,2,0:T(8,128)(2,1)}), bf16[4,8,3,2048]{3,1,2,0:T(8,128)(2,1)}, u32[]{:S(2)}, u32[]{:S(2)}) async-start(bf16[4,8,3,2048]{3,1,2,0:T(8,128)(2,1)} %copy.106), calls=%async_computation.2 | async-start | bytes 786432 | tf_op jit(solution)/shard_map/all_to_all | solution.py:105
  96.2 14.3 %copy-start.5 = (bf16[32,6,3,2048]{3,0,2,1:T(8,128)(2,1)S(1)}, bf16[32,6,3,2048]{3,0,2,1:T(8,128)(2,1)}, u32[]{:S(2)}) copy-start(bf16[32,6,3,2048]{3,0,2,1:T(8,128)(2,1)} %gather_fusion.5) | copy-start | bytes 7077892
  156.9 11.3 %copy-start.7 = (bf16[4,6,6,3,2048]{4,1,0,3,2:T(8,128)(2,1)S(1)}, bf16[4,6,6,3,2048]{4,1,0,3,2:T(8,128)(2,1)}, u32[]{:S(2)}) copy-start(bf16[4,6,6,3,2048]{4,1,0,3,2:T(8,128)(2,1)} %gather.47) | copy-start | bytes 5308420
  164.5 8.4 %all-to-all-start.4 = ((bf16[4,8,2048]{2,1,0:T(8,128)(2,1)}), bf16[4,8,2048]{2,1,0:T(8,128)(2,1)S(1)}, u32[]{:S(2)}, u32[]{:S(2)}) async-start(bf16[4,8,2048]{2,1,0:T(8,128)(2,1)} %fusion.16), calls=%async_computation.4 | async-start | bytes 262144 | tf_op jit(solution)/shard_map/all_to_all | solution.py:113
  172.9 46.8 %all-to-all-start = ((bf16[4,6,6,3,2048]{4,1,3,2,0:T(8,128)(2,1)}), bf16[4,6,6,3,2048]{4,1,3,2,0:T(8,128)(2,1)S(1)}, u32[]{:S(2)}, u32[]{:S(2)}) async-start(bf16[4,6,6,3,2048]{4,1,3,2,0:T(8,128)(2,1)} %copy.91), calls=%async_computation | async-start | bytes 4718592 | tf_op jit(solution)/shard_map/all_to_all | solution.py:86
  221.1 144.6 %all-to-all-start.1 = ((bf16[4,6,127,2048]{3,2,1,0:T(8,128)(2,1)}), bf16[4,6,127,2048]{3,2,1,0:T(8,128)(2,1)}, u32[]{:S(2)}, u32[]{:S(2)}) async-start(bf16[4,6,127,2048]{3,2,1,0:T(8,128)(2,1)} %broadcast_select_fusion.1), calls=%async_computation.1 | async-start | bytes 25165824 | tf_op jit(solution)/shard_map/all_to_all | solution.py:87
  228.4 7.0 %copy-start.27 = (s32[16]{0:T(128)S(1)}, s32[16]{0:T(128)}, u32[]{:S(2)}) copy-start(s32[16]{0:T(128)} %copy-done.26) | copy-start | bytes 196
  228.4 7.0 %copy-start.29 = (s32[12]{0:T(128)S(1)}, s32[12]{0:T(128)}, u32[]{:S(2)}) copy-start(s32[12]{0:T(128)} %param.11) | copy-start | bytes 148
  228.4 7.8 %copy-start.28 = (pred[16]{0:T(512)(128)(4,1)S(1)}, pred[16]{0:T(512)(128)(4,1)}, u32[]{:S(2)}) copy-start(pred[16]{0:T(512)(128)(4,1)} %get-tuple-element.2) | copy-start | bytes 52
  236.9 9.2 %copy-start.6 = (bf16[12,16,3,2048]{3,1,2,0:T(8,128)(2,1)S(1)}, bf16[12,16,3,2048]{3,1,2,0:T(8,128)(2,1)}, u32[]{:S(2)}) copy-start(bf16[12,16,3,2048]{3,1,2,0:T(8,128)(2,1)} %param.10) | copy-start | bytes 7077892
  246.1 4.2 copy-start.10
  246.2 4.2 copy-start.12
  246.2 4.2 copy-start.14
  246.2 4.2 copy-start.16
  246.2 4.2 copy-start.18
  246.2 4.2 copy-start.20
  374.5 12.6 %slice-start = ((s8[6291456]{0:T(1024)(128)(4,1)}), s8[2097152]{0:T(1024)(128)(4,1)S(1)}, s32[]{:S(2)}) async-start(s8[6291456]{0:T(1024)(128)(4,1)} %bitcast.90), calls=%async_computation.5 | async-start | bytes 4194304
  440.4 13.6 %copy-start.1 = (bf16[16,6,3,2048]{3,0,2,1:T(8,128)(2,1)S(1)}, bf16[16,6,3,2048]{3,0,2,1:T(8,128)(2,1)}, u32[]{:S(2)}) copy-start(bf16[16,6,3,2048]{3,0,2,1:T(8,128)(2,1)} %param.16) | copy-start | bytes 3538948
  (13 other events, 20.1 us)
where the time goes:
time: 464 us; the launch traced here: 454 us
  local copies, waits for them, and re-layouts  240 us (52%)
  waiting for transfers between devices  107 us (23%)
  other arithmetic  78.8 us (17%)
  starting transfers between devices  22.4 us (5%)
  matrix products  5.01 us (1%)
    all_to_all x1, waiting for transfers between devices, per_device(): lax.all_to_all(out_hist, 'ctx', split_axis=0, concat_axis=0, tiled=True)  104 us
    gather x2, local copies, waits for them, and re-layouts, per_device(): hist_state = jnp.take(cache_hist, flat_ids, axis=0)  56 us
    gather x2, local copies, waits for them, and re-layouts, per_device(): jnp.take(cache_hist, safe_slots, axis=0)  37.5 us
    transpose x2, other arithmetic, grouped_conv(): arranged.transpose(2, 1, 0, 3)  23.2 us
    convert_element_type x3, local copies, waits for them, and re-layouts, featurize(): product = (featured[:, :, 1] * featured[:, :, 2]).astype(jnp.bfloat16)  21.6 us
    transpose x2, local copies, waits for them, and re-layouts, grouped_conv(): arranged.transpose(2, 1, 0, 3)  18.7 us
    gather x2, local copies, waits for them, and re-layouts, per_device(): jnp.take(got_hist.reshape(peer_count * stretch_cap, hist_rows, channels),...  17.7 us
    select_n x1, other arithmetic, per_device(): hist_state = jnp.take(cache_hist, flat_ids, axis=0)  14.3 us
  transfers between devices with their start and end apart: 5, of which 2 were waited for; matrix products, arithmetic and copies ran while one was open for 38% of the time, Pallas kernels for 0%

commit v1 on v0

v1 whole, which is shorter than its diff:
```python
import functools

import jax
import jax.numpy as jnp
from jax import lax
from jax.experimental import pallas as pl
from jax.experimental.pallas import tpu as pltpu
from jax.sharding import PartitionSpec as P

LANES = 128
F32 = jnp.float32
BF16 = jnp.bfloat16


def round_up(value, unit):
    return (value + unit - 1) // unit * unit


def one_hot(left, right):
    return jnp.where(left == right, 1.0, 0.0).astype(BF16)


def dot(left, right):
    return jnp.dot(left, right, preferred_element_type=F32)


def iota(shape, axis):
    return lax.broadcasted_iota(jnp.int32, shape, axis)


def rank_of(owner_ref, index):
    rank = jnp.int32(0)
    for earlier in range(index):
        rank += (owner_ref[earlier] == owner_ref[index]).astype(jnp.int32)
    return rank


def pick_own_group(stacked, length, per_group):
    lane_group = lax.rem(iota((length, stacked.shape[1]), 1), LANES) // per_group
    picked = stacked[:length]
    for group in range(1, LANES // per_group):
        picked = jnp.where(lane_group == group, stacked[group * length : (group + 1) * length], picked)
    return picked


def pack_kernel(peers, cap, planes, slots, dpad, me_ref, slot_ref, owner_ref, code_ref, raw_ref, rows_ref, *rest):
    outs, (raw_sel, rows_sel) = rest[:peers], rest[peers:]
    padded = raw_sel.shape[0] // peers
    decode_count = owner_ref.shape[0]
    width = raw_ref.shape[1]

    @pl.when(pl.program_id(0) == 0)
    def _():
        row = iota((padded, 1), 0)
        column = iota((padded, planes * slots), 1)
        for k in range(peers):
            target = jnp.full((padded, 1), -1, jnp.int32)
            for r in range(cap):
                slot = jnp.maximum(slot_ref[0, me_ref[0] ^ k, r], 0)
                here = (row >= r * planes) & (row < (r + 1) * planes)
                target = jnp.where(here, (row - r * planes) * slots + slot, target)
            raw_sel[k * padded : (k + 1) * padded, :] = one_hot(column, target)
        lane = iota((1, 3 * decode_count), 1)
        target = jnp.zeros((1, 3 * decode_count), jnp.int32)
        for n in range(decode_count):
            base = (owner_ref[n] ^ me_ref[0]) * (3 * dpad) + rank_of(owner_ref, n)
            for s in range(3):
                target = jnp.where(lane == s * decode_count + n, base + s * dpad, target)
        rows_sel[...] = one_hot(iota(rows_sel.shape, 0), target)

    rows = dot(rows_sel[...], rows_ref[...])
    lane = iota((padded, width), 1)
    marked = iota((padded, width), 0) == cap * planes
    for k in range(peers):
        codes = jnp.full((padded, width), -1, jnp.int32)
        for n in range(decode_count):
            place = jnp.where(owner_ref[n] ^ me_ref[0] == k, rank_of(owner_ref, n), -1)
            codes = jnp.where(lane == place, code_ref[n], codes)
        raw = dot(raw_sel[k * padded : (k + 1) * padded, :], raw_ref[...])
        raw = jnp.where(marked, codes.astype(F32), raw)
        outs[k][...] = jnp.concatenate([raw, rows[k * 3 * dpad : (k + 1) * 3 * dpad]], axis=0).astype(BF16)


def history_kernel(peers, cap, length, per_group, me_ref, slot_ref, filter_ref, hist_ref, *rest):
    sends, (first_ref, taps_ref) = rest[:peers], rest[peers : peers + 2]
    stage, toeplitz, local, states = rest[peers + 2 :]
    hist_rows, slots, _ = hist_ref.shape
    groups, taps = filter_ref.shape
    tile_rows = LANES // per_group * length

    @pl.when(pl.program_id(0) == 0)
    def _():
        source, column = iota((taps, LANES), 0), iota((taps, LANES), 1)
        for i in range(length):
            shift = jnp.where(column < hist_rows, one_hot(source, taps - 1 + i - column).astype(F32), 0.0)
            stage[pl.ds(i, groups, stride=length), :] = dot(filter_ref[...], shift.astype(BF16))
        toeplitz[...] = stage[: groups * length, :].astype(BF16)
        for i in range(length):
            stage[pl.ds(i, groups, stride=length), :] = dot(filter_ref[...], one_hot(source, i - column))
        local[...] = stage[: groups * length, :].astype(BF16)

    start = pl.multiple_of(pl.program_id(0) * tile_rows, tile_rows)
    matrix = toeplitz[pl.ds(start, tile_rows), :]
    column0 = jnp.where(iota((LANES, LANES), 0) == 0, 1.0, 0.0).astype(BF16)
    taps_ref[...] = pick_own_group(dot(local[pl.ds(start, tile_rows), :], column0), length, per_group)
    stage[: hist_rows * slots, :] = hist_ref[...].astype(F32).reshape(hist_rows * slots, LANES)
    stage[hist_rows * slots : LANES * slots, :] = jnp.zeros(((LANES - hist_rows) * slots, LANES), F32)
    for slot in range(0, slots, 2):
        pair = jnp.concatenate([stage[pl.ds(slot + e, LANES, stride=slots), :] for e in range(2)], axis=1)
        picked = pick_own_group(dot(matrix, pair.astype(BF16)), length, per_group)
        for e in range(2):
            own = picked[:, e * LANES : (e + 1) * LANES]
            states[slot + e] = own.astype(BF16)
            first_ref[slot + e : slot + e + 1, :] = own[:1]
    for k in range(peers):
        for r in range(cap):
            sends[k][r] = states[jnp.maximum(slot_ref[0, me_ref[0] ^ k, r], 0)]


def decode_kernel(peers, staps, slots, dpad, mark, padded, weight_ref, raw_ref, first_ref, taps_ref, *rest):
    rows, codes, outs = rest[:peers], rest[peers : 2 * peers], rest[2 * peers :]
    lane = iota((slots, LANES), 0)
    selects = []
    for ref in codes:
        code = ref[...].astype(F32)[mark : mark + 1].astype(jnp.int32)
        selects.append(jnp.where(lane == code, 1.0, 0.0).T[:dpad])
    select = jnp.concatenate(selects, axis=0)
    arrived = [ref[...].astype(F32)[padded:] for ref in rows]
    weight = weight_ref[...].astype(F32)
    featured = []
    for s in range(3):
        own = jnp.concatenate([block[s * dpad : (s + 1) * dpad] for block in arrived], axis=0)
        value = weight[s, 0:1] * own
        for j in range(1, staps):
            plane = (staps - 1 - j) * 3 + s
            state = dot(select.astype(BF16), raw_ref[plane * slots : (plane + 1) * slots, :])
            value += weight[s, j : j + 1] * state
        featured.append(value)
    gated = (featured[1] * featured[2]).astype(BF16).astype(F32)
    history = jnp.dot(select, first_ref[...], preferred_element_type=F32, precision=lax.Precision.HIGHEST)
    result = featured[0] * (taps_ref[0:1, :] * gated + history)
    for k in range(peers):
        outs[k][...] = result[k * dpad : (k + 1) * dpad].astype(BF16)


def local_kernel(peers, planes, staps, per_group, me_ref, owner_ref, filter_ref, weight_ref, rows_ref, *rest):
    raws, (query_ref, conv_ref) = rest[:peers], rest[peers : peers + 2]
    select, stage, local, window = rest[peers + 2 :]
    count, _, length, _ = rows_ref.shape
    groups, taps = filter_ref.shape
    padded = select.shape[1] // peers
    tile_rows = LANES // per_group * length
    lead = 8
    span = lead + length

    @pl.when(pl.program_id(0) == 0)
    def _():
        source, column = iota((taps, LANES), 0), iota((taps, LANES), 1)
        for i in range(length):
            stage[pl.ds(i, groups, stride=length), :] = dot(filter_ref[...], one_hot(source, i - column))
        local[...] = stage[...].astype(BF16)
        row = iota((lead, 1), 0) - (lead - staps + 1)
        targets = []
        for c in range(count):
            base = (owner_ref[c] ^ me_ref[0]) * padded + rank_of(owner_ref, c) * planes
            targets += [jnp.where(row >= 0, base + row * 3 + s, -1) for s in range(3)]
        select[...] = one_hot(iota(select.shape, 1), jnp.concatenate(targets, axis=0))

    start = pl.multiple_of(pl.program_id(0) * tile_rows, tile_rows)
    matrix = local[pl.ds(start, tile_rows), :][:, :length]
    lead_rows = dot(select[...], jnp.concatenate([ref[...][:padded] for ref in raws], axis=0))
    weight = weight_ref[...].astype(F32)
    for first in range(0, count, 2):
        members = range(first, min(first + 2, count))
        products = []
        for c in members:
            featured = []
            for s in range(3):
                base = ((c % 2) * 3 + s) * span
                at = (c * 3 + s) * lead
                window[base : base + lead, :] = lead_rows[at : at + lead]
                window[base + lead : base + span, :] = rows_ref[c, s].astype(F32)
                value = weight[s, 0:1] * window[base + lead : base + span, :]
                for j in range(1, staps):
                    value += weight[s, j : j + 1] * window[base + lead - j : base + span - j, :]
                featured.append(value)
            query_ref[c] = featured[0]
            products.append((featured[1] * featured[2]).astype(BF16))
        picked = pick_own_group(dot(matrix, jnp.concatenate(products, axis=1)), length, per_group)
        for e, c in enumerate(members):
            conv_ref[c] = picked[:, e * LANES : (e + 1) * LANES]


def finish_kernel(peers, cap, dpad, me_ref, owner_ref, decode_owner_ref, query_ref, conv_ref, *rest):
    states, returned = rest[:peers], rest[peers : 2 * peers]
    out_ref, decode_ref, held = rest[2 * peers :]
    count = query_ref.shape[0]
    decode_count = decode_owner_ref.shape[0]
    for k in range(peers):
        for r in range(cap):
            held[k * cap + r] = states[k][r]
    for c in range(count):
        at = (owner_ref[c] ^ me_ref[0]) * cap + rank_of(owner_ref, c)
        out_ref[c] = (query_ref[c] * (conv_ref[c] + held[at].astype(F32))).astype(BF16)
    row = iota((decode_count, 1), 0)
    target = jnp.zeros((decode_count, 1), jnp.int32)
    for n in range(decode_count):
        at = (decode_owner_ref[n] ^ me_ref[0]) * dpad + rank_of(decode_owner_ref, n)
        target = jnp.where(row == n, at, target)
    select = one_hot(iota((decode_count, peers * dpad), 1), target)
    arrived = jnp.concatenate([ref[...].astype(F32) for ref in returned], axis=0).astype(BF16)
    decode_ref[...] = dot(select, arrived).astype(BF16)


def per_device(
    stretch_rows,
    stretch_owner,
    send_slot,
    decode_rows,
    row_owner,
    row_slot,
    cache_raw,
    cache_hist,
    short_weight,
    long_filter,
):
    peers = lax.axis_size("ctx")
    cap = send_slot.shape[2]
    count, length, _, channels = stretch_rows.shape
    slots, raw_rows, _, _ = cache_raw.shape
    hist_rows = cache_hist.shape[1]
    staps = short_weight.shape[0]
    groups, taps = long_filter.shape
    per_group = channels // groups
    decode_count = decode_rows.shape[0]
    dcap = max(2, (2 * decode_count + peers - 1) // peers)
    dpad = round_up(dcap, 8)
    planes = 3 * raw_rows
    padded = round_up(planes * cap + 1, 16)
    me = lax.axis_index("ctx").astype(jnp.int32).reshape(1)

    raw2d = cache_raw.transpose(1, 2, 0, 3).reshape(planes * slots, channels)
    hist3d = cache_hist.transpose(1, 0, 2)
    rows2d = decode_rows.transpose(1, 0, 2).reshape(3 * decode_count, channels)
    stretch = stretch_rows.transpose(0, 2, 1, 3)
    weight = short_weight.transpose(1, 0, 2)

    smem = pl.BlockSpec(memory_space=pltpu.SMEM)
    params = pltpu.CompilerParams(vmem_limit_bytes=48 * 1024 * 1024)

    def tiled(width, *lead):
        return pl.BlockSpec((*lead, width), lambda t: (0,) * len(lead) + (t,))

    def whole(*shape):
        return pl.BlockSpec(shape, lambda t: (0,) * len(shape))

    def cost(flops, data):
        return pl.CostEstimate(flops=flops, bytes_accessed=data, transcendentals=0)

    def send(array, k):
        return lax.ppermute(array, "ctx", [(i, i ^ k) for i in range(peers)])

    order = sorted(range(1, peers), reverse=True)
    width = min(512, channels)
    payload = padded + 3 * dpad
    sent = list(
        pl.pallas_call(
            functools.partial(pack_kernel, peers, cap, planes, slots, dpad),
            grid=(channels // width,),
            in_specs=[smem, smem, smem, smem, tiled(width, planes * slots), tiled(width, 3 * decode_count)],
            out_specs=[tiled(width, payload)] * peers,
            out_shape=[jax.ShapeDtypeStruct((payload, channels), BF16)] * peers,
            scratch_shapes=[
                pltpu.VMEM((peers * padded, planes * slots), BF16),
                pltpu.VMEM((peers * 3 * dpad, 3 * decode_count), BF16),
            ],
            compiler_params=params,
            cost_estimate=cost(2 * peers * padded * planes * slots * channels, 5 * planes * slots * channels),
        )(me, send_slot, row_owner, row_slot, raw2d, rows2d)
    )
    for k in order:
        sent[k] = send(sent[k], k)

    tile_rows = LANES // per_group * length
    history = pl.pallas_call(
        functools.partial(history_kernel, peers, cap, length, per_group),
        grid=(channels // LANES,),
        in_specs=[smem, smem, whole(groups, taps), tiled(LANES, hist_rows, slots)],
        out_specs=[tiled(LANES, cap, length)] * peers + [tiled(LANES, slots), tiled(LANES, length)],
        out_shape=[jax.ShapeDtypeStruct((cap, length, channels), BF16)] * peers
        + [jax.ShapeDtypeStruct((slots, channels), F32), jax.ShapeDtypeStruct((length, channels), F32)],
        scratch_shapes=[
            pltpu.VMEM((max(groups * length, LANES * slots), LANES), F32),
            pltpu.VMEM((groups * length, LANES), BF16),
            pltpu.VMEM((groups * length, LANES), BF16),
            pltpu.VMEM((slots, length, LANES), BF16),
        ],
        compiler_params=params,
        cost_estimate=cost(2 * slots * tile_rows * LANES * channels, 2 * hist_rows * slots * channels),
    )(me, send_slot, long_filter, hist3d)
    states, (first, expanded) = list(history[:peers]), history[peers:]
    for k in order:
        states[k] = send(states[k], k)

    returned = list(
        pl.pallas_call(
            functools.partial(decode_kernel, peers, staps, slots, dpad, planes * cap, padded),
            grid=(channels // width,),
            in_specs=[tiled(width, 3, staps), tiled(width, planes * slots), tiled(width, slots)]
            + [tiled(width, length)]
            + [tiled(width, payload)] * peers
            + [whole(payload, LANES)] * peers,
            out_specs=[tiled(width, dpad)] * peers,
            out_shape=[jax.ShapeDtypeStruct((dpad, channels), BF16)] * peers,
            compiler_params=params,
            cost_estimate=cost(2 * peers * dpad * planes * slots * channels, 4 * planes * slots * channels),
        )(weight, raw2d, first, expanded, *sent, *sent)
    )
    for k in order:
        returned[k] = send(returned[k], k)

    query, conv = pl.pallas_call(
        functools.partial(local_kernel, peers, planes, staps, per_group),
        grid=(channels // LANES,),
        in_specs=[smem, smem, whole(groups, taps), tiled(LANES, 3, staps), tiled(LANES, count, 3, length)]
        + [tiled(LANES, payload)] * peers,
        out_specs=[tiled(LANES, count, length)] * 2,
        out_shape=[jax.ShapeDtypeStruct((count, length, channels), F32)] * 2,
        scratch_shapes=[
            pltpu.VMEM((count * 3 * 8, peers * padded), BF16),
            pltpu.VMEM((groups * length, LANES), F32),
            pltpu.VMEM((groups * length, LANES), BF16),
            pltpu.VMEM((6 * (8 + length), LANES), F32),
        ],
        compiler_params=params,
        cost_estimate=cost(2 * count * 24 * peers * padded * channels, 14 * count * length * channels),
    )(me, stretch_owner, long_filter, weight, stretch, *sent)

    return pl.pallas_call(
        functools.partial(finish_kernel, peers, cap, dpad),
        grid=(channels // width,),
        in_specs=[smem, smem, smem]
        + [tiled(width, count, length)] * 2
        + [tiled(width, cap, length)] * peers
        + [tiled(width, dpad)] * peers,
        out_specs=[tiled(width, count, length), tiled(width, decode_count)],
        out_shape=[
            jax.ShapeDtypeStruct((count, length, channels), BF16),
            jax.ShapeDtypeStruct((decode_count, channels), BF16),
        ],
        scratch_shapes=[pltpu.VMEM((peers * cap, length, width), BF16)],
        compiler_params=params,
        cost_estimate=cost(3 * count * length * channels, 14 * count * length * channels),
    )(me, stretch_owner, row_owner, query, conv, *states, *returned)


def solution(mesh):
    placed = (
        P(("groups", "ctx"), None, None, "chan"),
        P(("groups", "ctx")),
        P(("groups", "ctx"), None, None),
        P(("groups", "ctx"), None, "chan"),
        P(("groups", "ctx")),
        P(("groups", "ctx")),
        P(("groups", "ctx"), None, None, "chan"),
        P(("groups", "ctx"), None, "chan"),
        P(None, None, "chan"),
        P("chan", None),
    )
    return jax.shard_map(
        per_device,
        mesh=mesh,
        in_specs=placed,
        out_specs=(P(("groups", "ctx"), None, "chan"), P(("groups", "ctx"), "chan")),
        check_vma=False,
    )
```

time: 464 us -> 59.9 us (0.13); the launches traced: 454 us -> 59.1 us
  local copies, waits for them, and re-layouts: 240 us -> 4.2 us
  waiting for transfers between devices: 107 us -> 6.81 us
  other arithmetic: 78.8 us -> 0 us
  Pallas kernels: 0 us -> 39.7 us
  starting transfers between devices: 22.4 us -> 7.72 us
  matrix products: 5.01 us -> 0 us
    gather x14 -> x0, local copies, waits for them, and re-layouts: 138 us -> none  [the longest x2 56 us: per_device(): hist_state = jnp.take(cache_hist, flat_ids, axis=0)]
    all_to_all x5 -> x0, waiting for transfers between devices: 107 us -> none  [the longest x1 104 us: per_device(): lax.all_to_all(out_hist, 'ctx', split_axis=0, concat_axis=0, tiled=True)]
    pallas_call x0 -> x5, Pallas kernels: none -> 39.7 us  [the longest x1 15.8 us: per_device(): pl.pallas_call(functools.partial(history_kernel, peers, cap, length, per_...]
    reshape x5 -> x0, local copies, waits for them, and re-layouts: 33.1 us -> none  [the longest x2 14.3 us: grouped_conv(): return convolved.reshape(row_count, length, channels)]
    transpose x4 -> x0, local copies, waits for them, and re-layouts: 29.6 us -> none  [the longest x2 18.7 us: grouped_conv(): arranged.transpose(2, 1, 0, 3)]
    select_n x10 -> x0, other arithmetic: 27.3 us -> none  [the longest x1 14.3 us: per_device(): hist_state = jnp.take(cache_hist, flat_ids, axis=0)]
    transpose x2 -> x0, other arithmetic: 23.2 us -> none  [grouped_conv(): arranged.transpose(2, 1, 0, 3)]
    all_to_all x5 -> x0, starting transfers between devices: 22.4 us -> none  [the longest x1 6.51 us: per_device(): lax.all_to_all(out_hist, 'ctx', split_axis=0, concat_axis=0, tiled=True)]
  transfers between devices with their start and end apart: 5 -> 9, of which waited for: 2 -> 1; matrix products, arithmetic and copies ran while one was open for 38% -> 0% of each run, Pallas kernels for 0% -> 54%
where the time goes in v1:
time: 59.9 us; the launch traced here: 59.1 us
  Pallas kernels  39.7 us (66%)
  starting transfers between devices  7.72 us (13%)
  waiting for transfers between devices  6.81 us (11%)
  local copies, waits for them, and re-layouts  4.2 us (7%)
  between operations  0.74 us (1%)
    pallas_call x1, Pallas kernels, per_device(): pl.pallas_call(functools.partial(history_kernel, peers, cap, length, per_...  15.8 us
    pallas_call x1, Pallas kernels, per_device(): pl.pallas_call(functools.partial(local_kernel, peers, planes, staps, per_...  14.2 us
    ppermute x9, starting transfers between devices, send(): return lax.ppermute(array, 'ctx', [(i, i ^ k) for i in range(peers)])  7.72 us
    ppermute x9, waiting for transfers between devices, send(): return lax.ppermute(array, 'ctx', [(i, i ^ k) for i in range(peers)])  6.81 us
    pallas_call x1, Pallas kernels, per_device(): pl.pallas_call(functools.partial(pack_kernel, peers, cap, planes, slots,...  4.4 us
    unnamed x18, local copies, waits for them, and re-layouts  4.2 us
    pallas_call x1, Pallas kernels, per_device(): pl.pallas_call(functools.partial(finish_kernel, peers, cap, dpad), grid=(...  3.16 us
    pallas_call x1, Pallas kernels, per_device(): pl.pallas_call(functools.partial(decode_kernel, peers, staps, slots, dpad...  2.1 us
  transfers between devices with their start and end apart: 9, of which 1 were waited for; matrix products, arithmetic and copies ran while one was open for 0% of the time, Pallas kernels for 54%

profile of v1, /device:TPU:0, one launch (start us, length us, event | category | flops | bytes accessed | tf_op | source)
XLA Modules:
  0.0 59.1 jit_solution(14178628235437344510)
XLA Ops:
  0.6 0.0 copy-start
  0.6 1.3 %copy-done = bf16[16,6,3,2048]{3,0,2,1:T(8,128)(2,1)S(1)} copy-done((bf16[16,6,3,2048]{3,0,2,1:T(8,128)(2,1)S(1)}, bf16[16,6,3,2048]{3,0,2,1:T(8,128)(2,1)}, u32[]{:S(2)}) %copy-start) | copy-done | bytes 1179672
  1.9 0.7 %copy-done.4 = s32[1,4,6]{2,1,0:T(4,128)S(1)} copy-done((s32[1,4,6]{2,1,0:T(4,128)S(1)}, s32[1,4,6]{2,1,0:T(4,128)}, u32[]{:S(2)}) %copy-start.4) | copy-done | bytes 120
  2.6 0.7 %copy-done.6 = s32[16]{0:T(128)S(1)} copy-done((s32[16]{0:T(128)S(1)}, s32[16]{0:T(128)}, u32[]{:S(2)}) %copy-start.6) | copy-done | bytes 88
  3.2 0.9 %copy-done.7 = bf16[16,3,2048]{2,0,1:T(8,128)(2,1)S(1)} copy-done((bf16[16,3,2048]{2,0,1:T(8,128)(2,1)S(1)}, bf16[16,3,2048]{2,0,1:T(8,128)(2,1)}, u32[]{:S(2)}) %copy-start.7) | copy-done | bytes 196632
  4.2 0.7 %copy-done.8 = s32[16]{0:T(128)S(1)} copy-done((s32[16]{0:T(128)S(1)}, s32[16]{0:T(128)}, u32[]{:S(2)}) %copy-start.8) | copy-done | bytes 88
  4.8 4.4 %shard_map.113 = (bf16[136,2048]{1,0:T(8,128)(2,1)S(1)}, bf16[136,2048]{1,0:T(8,128)(2,1)S(1)}, bf16[136,2048]{1,0:T(8,128)(2,1)S(1)}, bf16[136,2048]{1,0:T(8,128)(2,1)S(1)}) custom-call(s32[1]{0:T(128)} %bitcast.me_ref, s32[1,4,6]{2,1,0:T(4,128)S(1)} %copy-done.4, s32[16]{0:T(128)S(1)} %copy-done.6, s32[16]{0:T(128)S(1)} %copy-done.8, ...), custom_call_target="tpu_custom_call" | custom-call | flops 528482304 | bytes 2949120 | tf_op jit(solution)/shard_map/pallas_call | solution.py:267
  9.2 0.5 collective-permute-start
  9.8 2.6 %collective-permute-start.1 = (bf16[136,2048]{1,0:T(8,128)(2,1)S(1)}, bf16[136,2048]{1,0:T(8,128)(2,1)S(1)}, u32[]{:S(2)}, u32[]{:S(2)}) collective-permute-start(bf16[136,2048]{1,0:T(8,128)(2,1)S(1)} %get-tuple-element.20), channel_id=1, source_target_pairs={{0,8},{4,12},{8,0},{12,4},{1,9},{5,13},{9,1},{13,5},{2,10},{6,14},... | collective-permute-start | bytes 1671176 | tf_op jit(solution)/shard_map/ppermute | solution.py:261
  12.4 0.1 collective-permute-start.2
  12.4 15.8 %shard_map.115 = (bf16[6,16,2048]{2,1,0:T(8,128)(2,1)S(1)}, bf16[6,16,2048]{2,1,0:T(8,128)(2,1)S(1)}, bf16[6,16,2048]{2,1,0:T(8,128)(2,1)S(1)}, bf16[6,16,2048]{...) custom-call(s32[1]{0:T(128)} %bitcast.me_ref, s32[1,4,6]{2,1,0:T(4,128)S(1)} %copy-done.4, ...), custom_call_target="tpu_custom_call" | custom-call | flops 1073741824 | bytes 8323072 | tf_op jit(solution)/shard_map/pallas_call | solution.py:285
  28.3 0.2 collective-permute-start.3
  28.5 1.9 %collective-permute-start.4 = (bf16[6,16,2048]{2,1,0:T(8,128)(2,1)S(1)}, bf16[6,16,2048]{2,1,0:T(8,128)(2,1)S(1)}, u32[]{:S(2)}, u32[]{:S(2)}) collective-permute-start(bf16[6,16,2048]{2,1,0:T(8,128)(2,1)S(1)} %get-tuple-element.26), channel_id=1, source_target_pairs={{0,8},{4,12},{8,0},{12,4},{1,9},{5,13},{9,1},{13,5},{2,10},{6,14},... | collective-permute-start | bytes 1179656 | tf_op jit(solution)/shard_map/ppermute | solution.py:261
  30.4 0.0 collective-permute-done.rest_1_.rest_5_
  30.5 0.0 collective-permute-start.5
  30.5 0.0 collective-permute-done.1.rest_2_.rest_6_
  30.5 6.8 %collective-permute-done.2.rest_3_.rest_7_ = bf16[136,2048]{1,0:T(8,128)(2,1)S(1)} collective-permute-done((bf16[136,2048]{1,0:T(8,128)(2,1)S(1)}, bf16[136,2048]{1,0:T(8,128)(2,1)S(1)}, u32[]{:S(2)}, u32[]{:S(2)}) %collective-permute-start.2) | collective-permute-done | bytes 557088 | tf_op jit(solution)/shard_map/ppermute | solution.py:261
  37.3 2.1 %shard_map.116 = (bf16[8,2048]{1,0:T(8,128)(2,1)S(1)}, bf16[8,2048]{1,0:T(8,128)(2,1)S(1)}, bf16[8,2048]{1,0:T(8,128)(2,1)S(1)}, bf16[8,2048]{1,0:T(8,128)(2,1)S(1)}) custom-call(bf16[3,7,2048]{2,1,0:T(8,128)(2,1)S(1)} %bitcast.12, bf16[288,2048]{1,0:T(8,128)(2,1)S(1)} %bitcast.11, f32[16,2048]{1,0:T(8,128)S(1)} %get-tuple-element.28.first_ref, ...), custom_call_target="tpu_custom_call" | custom-call | flops 37748736 | bytes 2359296 | tf_op jit(solution)/shard_map/pallas_call | solution.py:306
  39.4 0.4 collective-permute-start.6
  39.8 1.9 %collective-permute-start.7 = (bf16[8,2048]{1,0:T(8,128)(2,1)S(1)}, bf16[8,2048]{1,0:T(8,128)(2,1)S(1)}, u32[]{:S(2)}, u32[]{:S(2)}) collective-permute-start(bf16[8,2048]{1,0:T(8,128)(2,1)S(1)} %get-tuple-element.32), channel_id=1, source_target_pairs={{0,8},{4,12},{8,0},{12,4},{1,9},{5,13},{9,1},{13,5},{2,10},{6,14},... | collective-permute-start | bytes 98312 | tf_op jit(solution)/shard_map/ppermute | solution.py:261
  41.7 14.2 %shard_map.114 = (f32[12,16,2048]{2,1,0:T(8,128)S(1)}, f32[12,16,2048]{2,1,0:T(8,128)S(1)}) custom-call(s32[1]{0:T(128)} %bitcast.me_ref, s32[12]{0:T(128)S(1)} %copy-done.5, bf16[128,128]{1,0:T(8,128)(2,1)S(1)} %copy-done.3, bf16[3,7,2048]{2,1,0:T(8,128)(2,1)S(1)} %bitcast.13, bf16[12,3,16,2048]{3,2,1,0:T(8,128)(2,1)} %bitcast.16, ...), custom_call_target="tpu_custom_call" | custom-call | flops 528482304 | bytes 5505024 | tf_op jit(solution)/shard_map/pallas_call | solution.py:322
  55.9 0.0 collective-permute-done.4.rest_2_
  55.9 0.0 collective-permute-done.6.rest_5_
  56.0 3.2 %shard_map.117 = (bf16[12,16,2048]{2,1,0:T(8,128)(2,1)}, bf16[16,2048]{1,0:T(8,128)(2,1)}) custom-call(s32[1]{0:T(128)} %bitcast.me_ref, s32[12]{0:T(128)S(1)} %copy-done.5, s32[16]{0:T(128)S(1)} %copy-done.6, f32[12,16,2048]{2,1,0:T(8,128)S(1)} %get-tuple-element.22.query_ref, f32[12,16,2048]{2,1,0:T(8,128)S(1)} %get-tuple-element.23.conv_ref, ...), custom_call_target="tpu_custom_call" | custom-call | flops 1179648 | bytes 5505024 | tf_op jit(solution)/shard_map/pallas_call | solution.py:339
  (17 shorter events, 0.0 us)
Async XLA Ops:
  0.6 1.3 %copy-start = (bf16[16,6,3,2048]{3,0,2,1:T(8,128)(2,1)S(1)}, bf16[16,6,3,2048]{3,0,2,1:T(8,128)(2,1)}, u32[]{:S(2)}) copy-start(bf16[16,6,3,2048]{3,0,2,1:T(8,128)(2,1)} %param.16) | copy-start | bytes 3538948
  1.9 0.7 %copy-start.4 = (s32[1,4,6]{2,1,0:T(4,128)S(1)}, s32[1,4,6]{2,1,0:T(4,128)}, u32[]{:S(2)}) copy-start(s32[1,4,6]{2,1,0:T(4,128)} %slot_ref.3) | copy-start | bytes 292
  2.6 0.7 %copy-start.6 = (s32[16]{0:T(128)S(1)}, s32[16]{0:T(128)}, u32[]{:S(2)}) copy-start(s32[16]{0:T(128)} %decode_owner_ref.1) | copy-start | bytes 196
  3.2 0.9 %copy-start.7 = (bf16[16,3,2048]{2,0,1:T(8,128)(2,1)S(1)}, bf16[16,3,2048]{2,0,1:T(8,128)(2,1)}, u32[]{:S(2)}) copy-start(bf16[16,3,2048]{2,0,1:T(8,128)(2,1)} %param.13) | copy-start | bytes 589828
  4.2 0.7 %copy-start.8 = (s32[16]{0:T(128)S(1)}, s32[16]{0:T(128)}, u32[]{:S(2)}) copy-start(s32[16]{0:T(128)} %code_ref.1) | copy-start | bytes 196
  4.8 7.6 %copy-start.3 = (bf16[128,128]{1,0:T(8,128)(2,1)S(1)}, bf16[128,128]{1,0:T(8,128)(2,1)}, u32[]{:S(2)}) copy-start(bf16[128,128]{1,0:T(8,128)(2,1)} %filter_ref.3) | copy-start | bytes 98308
  9.2 21.2 %collective-permute-start = (bf16[136,2048]{1,0:T(8,128)(2,1)S(1)}, bf16[136,2048]{1,0:T(8,128)(2,1)S(1)}, u32[]{:S(2)}, u32[]{:S(2)}) collective-permute-start(bf16[136,2048]{1,0:T(8,128)(2,1)S(1)} %get-tuple-element.19), channel_id=1, source_target_pairs={{0,4},{4,0},{8,12},{12,8},{1,5},{5,1},{9,13},{13,9},{2,6},{6,2},{1... | collective-permute-start | bytes 1671176 | tf_op jit(solution)/shard_map/ppermute | solution.py:261
  9.8 20.7 %collective-permute-start.1 = (bf16[136,2048]{1,0:T(8,128)(2,1)S(1)}, bf16[136,2048]{1,0:T(8,128)(2,1)S(1)}, u32[]{:S(2)}, u32[]{:S(2)}) collective-permute-start(bf16[136,2048]{1,0:T(8,128)(2,1)S(1)} %get-tuple-element.20), channel_id=1, source_target_pairs={{0,8},{4,12},{8,0},{12,4},{1,9},{5,13},{9,1},{13,5},{2,10},{6,14},... | collective-permute-start | bytes 1671176 | tf_op jit(solution)/shard_map/ppermute | solution.py:261
  12.4 24.9 %collective-permute-start.2 = (bf16[136,2048]{1,0:T(8,128)(2,1)S(1)}, bf16[136,2048]{1,0:T(8,128)(2,1)S(1)}, u32[]{:S(2)}, u32[]{:S(2)}) collective-permute-start(bf16[136,2048]{1,0:T(8,128)(2,1)S(1)} %get-tuple-element.21), channel_id=1, source_target_pairs={{0,12},{4,8},{8,4},{12,0},{1,13},{5,9},{9,5},{13,1},{2,14},{6,10},... | collective-permute-start | bytes 1671176 | tf_op jit(solution)/shard_map/ppermute | solution.py:261
  12.4 24.8 %copy-start.1 = (bf16[16,6,3,2048]{3,0,2,1:T(8,128)(2,1)S(1)}, bf16[16,6,3,2048]{3,0,2,1:T(8,128)(2,1)}, u32[]{:S(2)}) copy-start(bf16[16,6,3,2048]{3,0,2,1:T(8,128)(2,1)} %param.16) | copy-start | bytes 3538948
  12.4 24.8 %copy-start.2 = (bf16[7,3,2048]{2,0,1:T(8,128)(2,1)S(1)}, bf16[7,3,2048]{2,0,1:T(8,128)(2,1)}, u32[]{:S(2)}) copy-start(bf16[7,3,2048]{2,0,1:T(8,128)(2,1)} %param.18) | copy-start | bytes 258052
  28.3 13.5 %collective-permute-start.3 = (bf16[6,16,2048]{2,1,0:T(8,128)(2,1)S(1)}, bf16[6,16,2048]{2,1,0:T(8,128)(2,1)S(1)}, u32[]{:S(2)}, u32[]{:S(2)}) collective-permute-start(bf16[6,16,2048]{2,1,0:T(8,128)(2,1)S(1)} %get-tuple-element.25), channel_id=1, source_target_pairs={{0,4},{4,0},{8,12},{12,8},{1,5},{5,1},{9,13},{13,9},{2,6},{6,2},{1... | collective-permute-start | bytes 1179656 | tf_op jit(solution)/shard_map/ppermute | solution.py:261
  28.5 27.4 %collective-permute-start.4 = (bf16[6,16,2048]{2,1,0:T(8,128)(2,1)S(1)}, bf16[6,16,2048]{2,1,0:T(8,128)(2,1)S(1)}, u32[]{:S(2)}, u32[]{:S(2)}) collective-permute-start(bf16[6,16,2048]{2,1,0:T(8,128)(2,1)S(1)} %get-tuple-element.26), channel_id=1, source_target_pairs={{0,8},{4,12},{8,0},{12,4},{1,9},{5,13},{9,1},{13,5},{2,10},{6,14},... | collective-permute-start | bytes 1179656 | tf_op jit(solution)/shard_map/ppermute | solution.py:261
  30.5 25.5 %collective-permute-start.5 = (bf16[6,16,2048]{2,1,0:T(8,128)(2,1)S(1)}, bf16[6,16,2048]{2,1,0:T(8,128)(2,1)S(1)}, u32[]{:S(2)}, u32[]{:S(2)}) collective-permute-start(bf16[6,16,2048]{2,1,0:T(8,128)(2,1)S(1)} %get-tuple-element.27), channel_id=1, source_target_pairs={{0,12},{4,8},{8,4},{12,0},{1,13},{5,9},{9,5},{13,1},{2,14},{6,10},... | collective-permute-start | bytes 1179656 | tf_op jit(solution)/shard_map/ppermute | solution.py:261
  37.3 4.5 %copy-start.5 = (s32[12]{0:T(128)S(1)}, s32[12]{0:T(128)}, u32[]{:S(2)}) copy-start(s32[12]{0:T(128)} %owner_ref.5) | copy-start | bytes 148
  39.4 16.6 %collective-permute-start.6 = (bf16[8,2048]{1,0:T(8,128)(2,1)S(1)}, bf16[8,2048]{1,0:T(8,128)(2,1)S(1)}, u32[]{:S(2)}, u32[]{:S(2)}) collective-permute-start(bf16[8,2048]{1,0:T(8,128)(2,1)S(1)} %get-tuple-element.31), channel_id=1, source_target_pairs={{0,4},{4,0},{8,12},{12,8},{1,5},{5,1},{9,13},{13,9},{2,6},{6,2},{1... | collective-permute-start | bytes 98312 | tf_op jit(solution)/shard_map/ppermute | solution.py:261
  39.8 16.2 %collective-permute-start.7 = (bf16[8,2048]{1,0:T(8,128)(2,1)S(1)}, bf16[8,2048]{1,0:T(8,128)(2,1)S(1)}, u32[]{:S(2)}, u32[]{:S(2)}) collective-permute-start(bf16[8,2048]{1,0:T(8,128)(2,1)S(1)} %get-tuple-element.32), channel_id=1, source_target_pairs={{0,8},{4,12},{8,0},{12,4},{1,9},{5,13},{9,1},{13,5},{2,10},{6,14},... | collective-permute-start | bytes 98312 | tf_op jit(solution)/shard_map/ppermute | solution.py:261
  41.7 14.2 %collective-permute-start.8 = (bf16[8,2048]{1,0:T(8,128)(2,1)S(1)}, bf16[8,2048]{1,0:T(8,128)(2,1)S(1)}, u32[]{:S(2)}, u32[]{:S(2)}) collective-permute-start(bf16[8,2048]{1,0:T(8,128)(2,1)S(1)} %get-tuple-element.33), channel_id=1, source_target_pairs={{0,12},{4,8},{8,4},{12,0},{1,13},{5,9},{9,5},{13,1},{2,14},{6,10},... | collective-permute-start | bytes 98312 | tf_op jit(solution)/shard_map/ppermute | solution.py:261

commit v2 on v1

v2 whole, which is shorter than its diff:
```python
import functools

import jax
import jax.numpy as jnp
from jax import lax
from jax.experimental import pallas as pl
from jax.experimental.pallas import tpu as pltpu
from jax.sharding import PartitionSpec as P

LANES = 128
F32 = jnp.float32
BF16 = jnp.bfloat16


def round_up(value, unit):
    return (value + unit - 1) // unit * unit


def one_hot(left, right):
    return jnp.where(left == right, 1.0, 0.0).astype(BF16)


def dot(left, right):
    return jnp.dot(left, right, preferred_element_type=F32)


def iota(shape, axis):
    return lax.broadcasted_iota(jnp.int32, shape, axis)


def rank_of(owner_ref, index):
    rank = jnp.int32(0)
    for earlier in range(index):
        rank += (owner_ref[earlier] == owner_ref[index]).astype(jnp.int32)
    return rank


def pick_own_group(stacked, length, per_group):
    lane_group = lax.rem(iota((length, stacked.shape[1]), 1), LANES) // per_group
    picked = stacked[:length]
    for group in range(1, LANES // per_group):
        picked = jnp.where(lane_group == group, stacked[group * length : (group + 1) * length], picked)
    return picked


def pack_kernel(ks, cap, planes, slots, dpad, me_ref, slot_ref, owner_ref, code_ref, raw_hbm, rows_hbm, *rest):
    outs, (raw_ref, rows_ref, raw_sel, rows_sel, sems) = rest[: len(ks)], rest[len(ks) :]
    padded = raw_sel.shape[0] // len(ks)
    decode_count = owner_ref.shape[0]
    pairs = ((raw_hbm, raw_ref), (rows_hbm, rows_ref))
    copies = [pltpu.make_async_copy(source, target, sems.at[at]) for at, (source, target) in enumerate(pairs)]
    for copy in copies:
        copy.start()

    row = iota((padded, 1), 0)
    column = iota((padded, planes * slots), 1)
    lane = iota((1, 3 * decode_count), 1)
    wide = iota((1, LANES), 1)
    codes = []
    for at, k in enumerate(ks):
        peer = me_ref[0] ^ k
        target = jnp.full((padded, 1), -1, jnp.int32)
        for r in range(cap):
            slot = jnp.maximum(slot_ref[0, peer, r], 0)
            here = (row >= r * planes) & (row < (r + 1) * planes)
            target = jnp.where(here, (row - r * planes) * slots + slot, target)
        raw_sel[at * padded : (at + 1) * padded, :] = one_hot(column, target)
        target = jnp.full((1, 3 * decode_count), -1, jnp.int32)
        code = jnp.full((1, LANES), -1, jnp.int32)
        rank = jnp.int32(0)
        for n in range(decode_count):
            mine = owner_ref[n] == peer
            for s in range(3):
                hit = jnp.where(mine, s * decode_count + n, -1)
                target = jnp.where(lane == hit, rank + s * dpad, target)
            code = jnp.where(wide == jnp.where(mine, rank, -1), code_ref[n], code)
            rank += mine.astype(jnp.int32)
        rows_sel[at] = one_hot(iota(rows_sel.shape[1:], 0), target)
        codes.append(code.astype(F32))

    for copy in copies:
        copy.wait()
    marked = iota((padded, LANES), 0) == cap * planes
    for at in range(len(ks)):
        raw = dot(raw_sel[at * padded : (at + 1) * padded, :], raw_ref[...])
        head = jnp.where(marked, codes[at], raw[:, :LANES])
        raw = jnp.concatenate([head, raw[:, LANES:]], axis=1)
        outs[at][...] = jnp.concatenate([raw, dot(rows_sel[at], rows_ref[...])], axis=0).astype(BF16)


def history_kernel(peers, cap, length, per_group, me_ref, slot_ref, filter_ref, hist_ref, *rest):
    sends, (first_ref, taps_ref) = rest[:peers], rest[peers : peers + 2]
    stage, toeplitz, local, states = rest[peers + 2 :]
    hist_rows, slots, _ = hist_ref.shape
    groups, taps = filter_ref.shape
    tile_rows = LANES // per_group * length

    @pl.when(pl.program_id(0) == 0)
    def _():
        source, column = iota((taps, LANES), 0), iota((taps, LANES), 1)
        for i in range(length):
            shift = jnp.where(column < hist_rows, one_hot(source, taps - 1 + i - column).astype(F32), 0.0)
            stage[pl.ds(i, groups, stride=length), :] = dot(filter_ref[...], shift.astype(BF16))
        toeplitz[...] = stage[: groups * length, :].astype(BF16)
        for i in range(length):
            stage[pl.ds(i, groups, stride=length), :] = dot(filter_ref[...], one_hot(source, i - column))
        local[...] = stage[: groups * length, :].astype(BF16)

    column0 = jnp.where(iota((LANES, LANES), 0) == 0, 1.0, 0.0).astype(BF16)
    tiles = hist_ref.shape[2] // LANES
    for tile in range(tiles):
        start = pl.multiple_of((pl.program_id(0) * tiles + tile) * tile_rows, tile_rows)
        lanes = slice(tile * LANES, (tile + 1) * LANES)
        expanded = dot(local[pl.ds(start, tile_rows), :], column0)
        taps_ref[:, lanes] = pick_own_group(expanded, length, per_group)
        matrix = toeplitz[pl.ds(start, tile_rows), :]
        block = hist_ref[:, :, lanes]
        rest_rows = jnp.zeros((LANES - hist_rows, slots, LANES), BF16)
        by_slot = jnp.swapaxes(jnp.concatenate([block, rest_rows], axis=0), 0, 1)
        for slot in range(0, slots, 2):
            pair = jnp.concatenate([by_slot[slot], by_slot[slot + 1]], axis=1)
            picked = pick_own_group(dot(matrix, pair), length, per_group)
            for e in range(2):
                own = picked[:, e * LANES : (e + 1) * LANES]
                states[slot + e, :, lanes] = own.astype(BF16)
                first_ref[slot + e : slot + e + 1, lanes] = own[:1]
    for k in range(peers):
        for r in range(cap):
            sends[k][r] = states[jnp.maximum(slot_ref[0, me_ref[0] ^ k, r], 0)]


def decode_kernel(peers, staps, slots, dpad, mark, padded, weight_ref, raw_ref, first_ref, taps_ref, *rest):
    rows, codes, outs = rest[:peers], rest[peers : 2 * peers], rest[2 * peers :]
    lane = iota((slots, LANES), 0)
    selects = []
    for ref in codes:
        code = ref[...].astype(F32)[mark : mark + 1].astype(jnp.int32)
        selects.append(jnp.where(lane == code, 1.0, 0.0).T[:dpad])
    select = jnp.concatenate(selects, axis=0)
    arrived = [ref[...].astype(F32)[padded:] for ref in rows]
    weight = weight_ref[...].astype(F32)
    featured = []
    for s in range(3):
        own = jnp.concatenate([block[s * dpad : (s + 1) * dpad] for block in arrived], axis=0)
        value = weight[s, 0:1] * own
        for j in range(1, staps):
            plane = (staps - 1 - j) * 3 + s
            state = dot(select.astype(BF16), raw_ref[plane * slots : (plane + 1) * slots, :])
            value += weight[s, j : j + 1] * state
        featured.append(value)
    gated = (featured[1] * featured[2]).astype(BF16).astype(F32)
    history = jnp.dot(select, first_ref[...], preferred_element_type=F32, precision=lax.Precision.HIGHEST)
    result = featured[0] * (taps_ref[0:1, :] * gated + history)
    for k in range(peers):
        outs[k][...] = result[k * dpad : (k + 1) * dpad].astype(BF16)


def local_kernel(peers, planes, staps, per_group, me_ref, owner_ref, filter_ref, weight_ref, rows_ref, *rest):
    raws, (query_ref, conv_ref) = rest[:peers], rest[peers : peers + 2]
    select, stage, local, window = rest[peers + 2 :]
    count, _, length, _ = rows_ref.shape
    groups, taps = filter_ref.shape
    padded = select.shape[1] // peers
    tile_rows = LANES // per_group * length
    lead = 8
    span = lead + length

    @pl.when(pl.program_id(0) == 0)
    def _():
        source, column = iota((taps, LANES), 0), iota((taps, LANES), 1)
        for i in range(length):
            stage[pl.ds(i, groups, stride=length), :] = dot(filter_ref[...], one_hot(source, i - column))
        local[...] = stage[...].astype(BF16)
        row = iota((lead, 1), 0) - (lead - staps + 1)
        targets = []
        for c in range(count):
            base = (owner_ref[c] ^ me_ref[0]) * padded + rank_of(owner_ref, c) * planes
            targets += [jnp.where(row >= 0, base + row * 3 + s, -1) for s in range(3)]
        select[...] = one_hot(iota(select.shape, 1), jnp.concatenate(targets, axis=0))

    lead_rows = dot(select[...], jnp.concatenate([ref[...][:padded] for ref in raws], axis=0))
    weights = weight_ref[...].astype(F32)
    tiles = rows_ref.shape[3] // LANES
    for tile in range(tiles):
        start = pl.multiple_of((pl.program_id(0) * tiles + tile) * tile_rows, tile_rows)
        lanes = slice(tile * LANES, (tile + 1) * LANES)
        matrix = local[pl.ds(start, tile_rows), :][:, :length]
        weight = weights[:, :, lanes]
        for first in range(0, count, 2):
            members = range(first, min(first + 2, count))
            products = []
            for c in members:
                featured = []
                for s in range(3):
                    base = (((tile % 2) * count + c) * 3 + s) * span
                    at = (c * 3 + s) * lead
                    window[base : base + lead, :] = lead_rows[at : at + lead, lanes]
                    window[base + lead : base + span, :] = rows_ref[c, s, :, lanes].astype(F32)
                    value = weight[s, 0:1] * window[base + lead : base + span, :]
                    for j in range(1, staps):
                        value += weight[s, j : j + 1] * window[base + lead - j : base + span - j, :]
                    featured.append(value)
                query_ref[c, :, lanes] = featured[0]
                products.append((featured[1] * featured[2]).astype(BF16))
            picked = pick_own_group(dot(matrix, jnp.concatenate(products, axis=1)), length, per_group)
            for e, c in enumerate(members):
                conv_ref[c, :, lanes] = picked[:, e * LANES : (e + 1) * LANES]


def finish_kernel(peers, cap, dpad, me_ref, owner_ref, decode_owner_ref, query_ref, conv_ref, *rest):
    states, returned = rest[:peers], rest[peers : 2 * peers]
    out_ref, decode_ref, held, places, select = rest[2 * peers :]
    count, length, width = out_ref.shape
    decode_count = decode_owner_ref.shape[0]

    @pl.when(pl.program_id(0) == 0)
    def _():
        for c in range(count):
            places[c] = (owner_ref[c] ^ me_ref[0]) * cap + rank_of(owner_ref, c)
        row = iota((decode_count, 1), 0)
        target = jnp.zeros((decode_count, 1), jnp.int32)
        for n in range(decode_count):
            at = (decode_owner_ref[n] ^ me_ref[0]) * dpad + rank_of(decode_owner_ref, n)
            target = jnp.where(row == n, at, target)
        select[...] = one_hot(iota((decode_count, peers * dpad), 1), target)

    lanes = pl.ds(pl.multiple_of(pl.program_id(0) * width, width), width)
    for k in range(peers):
        for r in range(cap):
            held[k * cap + r] = states[k][r, :, lanes]
    for c in range(count):
        state = held[places[c]].astype(F32)
        out_ref[c] = (query_ref[c, :, lanes] * (conv_ref[c, :, lanes] + state)).astype(BF16)
    arrived = jnp.concatenate([ref[:, lanes].astype(F32) for ref in returned], axis=0).astype(BF16)
    decode_ref[...] = dot(select[...], arrived).astype(BF16)


def per_device(
    stretch_rows,
    stretch_owner,
    send_slot,
    decode_rows,
    row_owner,
    row_slot,
    cache_raw,
    cache_hist,
    short_weight,
    long_filter,
):
    peers = lax.axis_size("ctx")
    cap = send_slot.shape[2]
    count, length, _, channels = stretch_rows.shape
    slots, raw_rows, _, _ = cache_raw.shape
    hist_rows = cache_hist.shape[1]
    staps = short_weight.shape[0]
    groups, taps = long_filter.shape
    per_group = channels // groups
    decode_count = decode_rows.shape[0]
    dcap = max(2, (2 * decode_count + peers - 1) // peers)
    dpad = round_up(dcap, 8)
    planes = 3 * raw_rows
    padded = round_up(planes * cap + 1, 16)
    me = lax.axis_index("ctx").astype(jnp.int32).reshape(1)

    raw2d = cache_raw.transpose(1, 2, 0, 3).reshape(planes * slots, channels)
    hist3d = cache_hist.transpose(1, 0, 2)
    rows2d = decode_rows.transpose(1, 0, 2).reshape(3 * decode_count, channels)
    stretch = stretch_rows.transpose(0, 2, 1, 3)
    weight = short_weight.transpose(1, 0, 2)

    smem = pl.BlockSpec(memory_space=pltpu.SMEM)
    vmem = pl.BlockSpec(memory_space=pltpu.VMEM)
    hbm = pl.BlockSpec(memory_space=pltpu.HBM)
    params = pltpu.CompilerParams(vmem_limit_bytes=32 * 1024 * 1024)

    def tiled(width, *lead):
        return pl.BlockSpec((*lead, width), lambda t: (0,) * len(lead) + (t,))

    def whole(*shape):
        return pl.BlockSpec(shape, lambda t: (0,) * len(shape))

    def cost(flops, data):
        return pl.CostEstimate(flops=1, bytes_accessed=1, transcendentals=0)

    def send(array, k):
        return lax.ppermute(array, "ctx", [(i, i ^ k) for i in range(peers)])

    order = sorted(range(1, peers), reverse=True)
    width = min(512, channels)
    payload = padded + 3 * dpad
    sent = [None] * peers

    def pack(ks, limit, raw_in, rows_in):
        packed = pl.pallas_call(
            functools.partial(pack_kernel, ks, cap, planes, slots, dpad),
            in_specs=[smem] * 4 + [hbm] * 2,
            out_specs=[vmem] * len(ks),
            out_shape=[jax.ShapeDtypeStruct((payload, channels), BF16)] * len(ks),
            scratch_shapes=[
                pltpu.VMEM((planes * slots, channels), BF16),
                pltpu.VMEM((3 * decode_count, channels), BF16),
                pltpu.VMEM((len(ks) * padded, planes * slots), BF16),
                pltpu.VMEM((len(ks), 3 * dpad, 3 * decode_count), BF16),
                pltpu.SemaphoreType.DMA((2,)),
            ],
            compiler_params=pltpu.CompilerParams(vmem_limit_bytes=limit * 1024 * 1024),
            cost_estimate=cost(2 * len(ks) * padded * planes * slots * channels, 4 * planes * slots * channels),
        )(me, send_slot, row_owner, row_slot, raw_in, rows_in)
        for k, block in zip(ks, packed):
            sent[k] = send(block, k) if k else block

    pack(order[:-1], 60, raw2d, rows2d)

    tile_rows = LANES // per_group * length
    history = pl.pallas_call(
        functools.partial(history_kernel, peers, cap, length, per_group),
        grid=(channels // width,),
        in_specs=[smem, smem, whole(groups, taps), tiled(width, hist_rows, slots)],
        out_specs=[tiled(width, cap, length)] * peers + [tiled(width, slots), tiled(width, length)],
        out_shape=[jax.ShapeDtypeStruct((cap, length, channels), BF16)] * peers
        + [jax.ShapeDtypeStruct((slots, channels), F32), jax.ShapeDtypeStruct((length, channels), F32)],
        scratch_shapes=[
            pltpu.VMEM((groups * length, LANES), F32),
            pltpu.VMEM((groups * length, LANES), BF16),
            pltpu.VMEM((groups * length, LANES), BF16),
            pltpu.VMEM((slots, length, width), BF16),
        ],
        compiler_params=pltpu.CompilerParams(vmem_limit_bytes=48 * 1024 * 1024),
        cost_estimate=cost(2 * slots * tile_rows * LANES * channels, 2 * hist_rows * slots * channels),
    )(me, send_slot, long_filter, hist3d)
    states, (first, expanded) = list(history[:peers]), history[peers:]
    raw_in, rows_in, first = lax.optimization_barrier((raw2d, rows2d, first))
    pack([1, 0], 32, raw_in, rows_in)
    for k in order:
        states[k] = send(states[k], k)

    returned = list(
        pl.pallas_call(
            functools.partial(decode_kernel, peers, staps, slots, dpad, planes * cap, padded),
            grid=(channels // width,),
            in_specs=[tiled(width, 3, staps), tiled(width, planes * slots), tiled(width, slots)]
            + [tiled(width, length)]
            + [tiled(width, payload)] * peers
            + [whole(payload, LANES)] * peers,
            out_specs=[tiled(width, dpad)] * peers,
            out_shape=[jax.ShapeDtypeStruct((dpad, channels), BF16)] * peers,
            compiler_params=params,
            cost_estimate=cost(2 * peers * dpad * planes * slots * channels, 4 * planes * slots * channels),
        )(weight, raw2d, first, expanded, *sent, *sent)
    )
    for k in order:
        returned[k] = send(returned[k], k)

    query, conv = pl.pallas_call(
        functools.partial(local_kernel, peers, planes, staps, per_group),
        grid=(channels // width,),
        in_specs=[smem, smem, whole(groups, taps), tiled(width, 3, staps), tiled(width, count, 3, length)]
        + [tiled(width, payload)] * peers,
        out_specs=[tiled(width, count, length)] * 2,
        out_shape=[jax.ShapeDtypeStruct((count, length, channels), F32)] * 2,
        scratch_shapes=[
            pltpu.VMEM((count * 3 * 8, peers * padded), BF16),
            pltpu.VMEM((groups * length, LANES), F32),
            pltpu.VMEM((groups * length, LANES), BF16),
            pltpu.VMEM((2 * count * 3 * (8 + length), LANES), F32),
        ],
        compiler_params=params,
        cost_estimate=cost(2 * count * 24 * peers * padded * channels, 14 * count * length * channels),
    )(me, stretch_owner, long_filter, weight, stretch, *sent)

    return pl.pallas_call(
        functools.partial(finish_kernel, peers, cap, dpad),
        grid=(channels // width,),
        in_specs=[smem, smem, smem] + [vmem] * (2 + 2 * peers),
        out_specs=[tiled(width, count, length), tiled(width, decode_count)],
        out_shape=[
            jax.ShapeDtypeStruct((count, length, channels), BF16),
            jax.ShapeDtypeStruct((decode_count, channels), BF16),
        ],
        scratch_shapes=[
            pltpu.VMEM((peers * cap, length, width), BF16),
            pltpu.SMEM((count,), jnp.int32),
            pltpu.VMEM((decode_count, peers * dpad), BF16),
        ],
        compiler_params=params,
        cost_estimate=cost(3 * count * length * channels, 14 * count * length * channels),
    )(me, stretch_owner, row_owner, query, conv, *states, *returned)


def solution(mesh):
    placed = (
        P(("groups", "ctx"), None, None, "chan"),
        P(("groups", "ctx")),
        P(("groups", "ctx"), None, None),
        P(("groups", "ctx"), None, "chan"),
        P(("groups", "ctx")),
        P(("groups", "ctx")),
        P(("groups", "ctx"), None, None, "chan"),
        P(("groups", "ctx"), None, "chan"),
        P(None, None, "chan"),
        P("chan", None),
    )
    return jax.shard_map(
        per_device,
        mesh=mesh,
        in_specs=placed,
        out_specs=(P(("groups", "ctx"), None, "chan"), P(("groups", "ctx"), "chan")),
        check_vma=False,
    )
```

time: 59.9 us -> 52.8 us (0.88)
  Pallas kernels: 39.7 us -> 25.4 us
  waiting for transfers between devices: 6.81 us -> 17.2 us
  local copies, waits for them, and re-layouts: 4.2 us -> 1.47 us
    ppermute x9, waiting for transfers between devices: 6.81 us -> 17.2 us  [send(): return lax.ppermute(array, 'ctx', [(i, i ^ k) for i in range(peers)])]
    pallas_call x1, Pallas kernels: 14.2 us -> 6.65 us  [per_device(): pl.pallas_call(functools.partial(local_kernel, peers, planes, staps, per_...]
    pallas_call x1, Pallas kernels: 15.8 us -> 8.44 us  [per_device(): pl.pallas_call(functools.partial(history_kernel, peers, cap, length, per_...]
    unnamed x18, local copies, waits for them, and re-layouts: 4.2 us -> 1.47 us
    pallas_call x1 -> x2, Pallas kernels: 4.4 us -> 5.73 us  [pack(): pl.pallas_call(functools.partial(pack_kernel, ks, cap, planes, slots, dpa...]
    pallas_call x1, Pallas kernels: 3.16 us -> 2.53 us  [per_device(): pl.pallas_call(functools.partial(finish_kernel, peers, cap, dpad), grid=(...]
  transfers between devices with their start and end apart: 9 -> 9, of which waited for: 1 -> 3; matrix products, arithmetic and copies ran while one was open for 0% -> 0% of each run, Pallas kernels for 54% -> 37%
where the time goes in v2:
time: 52.8 us; the launch traced here: 52.5 us
  Pallas kernels  25.4 us (48%)
  waiting for transfers between devices  17.2 us (33%)
  starting transfers between devices  7.65 us (14%)
  local copies, waits for them, and re-layouts  1.47 us (3%)
  between operations  0.75 us (1%)
    ppermute x9, waiting for transfers between devices, send(): return lax.ppermute(array, 'ctx', [(i, i ^ k) for i in range(peers)])  17.2 us
    pallas_call x1, Pallas kernels, per_device(): pl.pallas_call(functools.partial(history_kernel, peers, cap, length, per_...  8.44 us
    ppermute x9, starting transfers between devices, send(): return lax.ppermute(array, 'ctx', [(i, i ^ k) for i in range(peers)])  7.65 us
    pallas_call x1, Pallas kernels, per_device(): pl.pallas_call(functools.partial(local_kernel, peers, planes, staps, per_...  6.65 us
    pallas_call x2, Pallas kernels, pack(): pl.pallas_call(functools.partial(pack_kernel, ks, cap, planes, slots, dpa...  5.73 us
    pallas_call x1, Pallas kernels, per_device(): pl.pallas_call(functools.partial(finish_kernel, peers, cap, dpad), grid=(...  2.53 us
    pallas_call x1, Pallas kernels, per_device(): pl.pallas_call(functools.partial(decode_kernel, peers, staps, slots, dpad...  2.1 us
    unnamed x18, local copies, waits for them, and re-layouts  1.47 us
  transfers between devices with their start and end apart: 9, of which 3 were waited for; matrix products, arithmetic and copies ran while one was open for 0% of the time, Pallas kernels for 37%

profile of v2, /device:TPU:0, one launch (start us, length us, event | category | flops | bytes accessed | tf_op | source)
XLA Modules:
  0.0 52.5 jit_solution(16944983397113454725)
XLA Ops:
  0.6 3.6 %shard_map.115 = (bf16[136,2048]{1,0:T(8,128)(2,1)}, bf16[136,2048]{1,0:T(8,128)(2,1)}) custom-call(s32[1]{0:T(128)} %bitcast.me_ref, s32[1,4,6]{2,1,0:T(4,128)} %slot_ref.5, s32[16]{0:T(128)} %decode_owner_ref.1, s32[16]{0:T(128)} %code_ref.3, bf16[288,2048]{1,0:T(8,128)(2,1)} %bitcast.10, bf16[48,2048]{1,0:T(8,128)(2,1)} %bitcast.14), custom_call_target="tpu_custom_call" | custom-call | flops 1 | bytes 1 | tf_op jit(solution)/shard_map/pallas_call | solution.py:294
  4.3 3.0 %collective-permute-start.1 = (bf16[136,2048]{1,0:T(8,128)(2,1)}, bf16[136,2048]{1,0:T(8,128)(2,1)S(1)}, u32[]{:S(2)}, u32[]{:S(2)}) collective-permute-start(bf16[136,2048]{1,0:T(8,128)(2,1)} %get-tuple-element.26), channel_id=1, source_target_pairs={{0,8},{4,12},{8,0},{12,4},{1,9},{5,13},{9,1},{13,5},{2,10},{6,14},... | collective-permute-start | bytes 1671176 | tf_op jit(solution)/shard_map/ppermute | solution.py:286
  7.3 0.0 collective-permute-start.2
  7.3 0.8 %copy-done.4 = bf16[128,128]{1,0:T(8,128)(2,1)S(1)} copy-done((bf16[128,128]{1,0:T(8,128)(2,1)S(1)}, bf16[128,128]{1,0:T(8,128)(2,1)}, u32[]{:S(2)}) %copy-start.4) | copy-done | bytes 32792
  8.1 0.7 %copy-done.5 = s32[1,4,6]{2,1,0:T(4,128)S(1)} copy-done((s32[1,4,6]{2,1,0:T(4,128)S(1)}, s32[1,4,6]{2,1,0:T(4,128)}, u32[]{:S(2)}) %copy-start.5) | copy-done | bytes 120
  8.8 0.0 copy-start.3
  8.8 8.4 %shard_map.113 = (bf16[6,16,2048]{2,1,0:T(8,128)(2,1)S(1)}, bf16[6,16,2048]{2,1,0:T(8,128)(2,1)S(1)}, bf16[6,16,2048]{2,1,0:T(8,128)(2,1)S(1)}, bf16[6,16,2048]{...) custom-call(s32[1]{0:T(128)} %bitcast.me_ref, s32[1,4,6]{2,1,0:T(4,128)S(1)} %copy-done.5, ...), custom_call_target="tpu_custom_call" | custom-call | flops 1 | bytes 1 | tf_op jit(solution)/shard_map/pallas_call | solution.py:315
  17.3 2.1 %shard_map.114 = (bf16[136,2048]{1,0:T(8,128)(2,1)S(1)}, bf16[136,2048]{1,0:T(8,128)(2,1)S(1)}) custom-call(s32[1]{0:T(128)} %bitcast.me_ref, s32[1,4,6]{2,1,0:T(4,128)S(1)} %copy-done.5, s32[16]{0:T(128)S(1)} %copy-done.6, s32[16]{0:T(128)S(1)} %copy-done.7, bf16[288,2048]{1,0:T(8,128)(2,1)S(1)} %bitcast.11, bf16[48,2048]{1,0:T(8,128)(2,1)S(1)} %bitcast.15), custom_call_target="tpu_custom_call" | custom-call | flops 1 | bytes 1 | tf_op jit(solution)/shard_map/pallas_call | solution.py:294
  19.4 0.2 collective-permute-start
  19.6 0.3 collective-permute-start.3
  19.9 1.7 %collective-permute-start.4 = (bf16[6,16,2048]{2,1,0:T(8,128)(2,1)S(1)}, bf16[6,16,2048]{2,1,0:T(8,128)(2,1)S(1)}, u32[]{:S(2)}, u32[]{:S(2)}) collective-permute-start(bf16[6,16,2048]{2,1,0:T(8,128)(2,1)S(1)} %get-tuple-element.32), channel_id=1, source_target_pairs={{0,8},{4,12},{8,0},{12,4},{1,9},{5,13},{9,1},{13,5},{2,10},{6,14},... | collective-permute-start | bytes 1179656 | tf_op jit(solution)/shard_map/ppermute | solution.py:286
  21.7 0.1 collective-permute-start.5
  21.7 10.9 %collective-permute-done.2.rest_3_.rest_7_ = bf16[136,2048]{1,0:T(8,128)(2,1)S(1)} collective-permute-done((bf16[136,2048]{1,0:T(8,128)(2,1)}, bf16[136,2048]{1,0:T(8,128)(2,1)S(1)}, u32[]{:S(2)}, u32[]{:S(2)}) %collective-permute-start.2) | collective-permute-done | bytes 557088 | tf_op jit(solution)/shard_map/ppermute | solution.py:286
  32.6 2.1 %shard_map.117 = (bf16[8,2048]{1,0:T(8,128)(2,1)S(1)}, bf16[8,2048]{1,0:T(8,128)(2,1)S(1)}, bf16[8,2048]{1,0:T(8,128)(2,1)S(1)}, bf16[8,2048]{1,0:T(8,128)(2,1)S(1)}) custom-call(bf16[3,7,2048]{2,1,0:T(8,128)(2,1)S(1)} %bitcast.16, bf16[288,2048]{1,0:T(8,128)(2,1)S(1)} %bitcast.12, f32[16,2048]{1,0:T(8,128)S(1)} %get-tuple-element.34.first_ref, ...), custom_call_target="tpu_custom_call" | custom-call | flops 1 | bytes 1 | tf_op jit(solution)/shard_map/pallas_call | solution.py:338
  34.7 0.2 collective-permute-start.6
  34.9 2.1 %collective-permute-start.7 = (bf16[8,2048]{1,0:T(8,128)(2,1)S(1)}, bf16[8,2048]{1,0:T(8,128)(2,1)S(1)}, u32[]{:S(2)}, u32[]{:S(2)}) collective-permute-start(bf16[8,2048]{1,0:T(8,128)(2,1)S(1)} %get-tuple-element.38), channel_id=1, source_target_pairs={{0,8},{4,12},{8,0},{12,4},{1,9},{5,13},{9,1},{13,5},{2,10},{6,14},... | collective-permute-start | bytes 98312 | tf_op jit(solution)/shard_map/ppermute | solution.py:286
  37.0 0.0 collective-permute-done.3.rest_1_
  37.0 0.0 collective-permute-start.8
  37.0 6.6 %shard_map.116 = (f32[12,16,2048]{2,1,0:T(8,128)S(1)}, f32[12,16,2048]{2,1,0:T(8,128)S(1)}) custom-call(s32[1]{0:T(128)} %bitcast.me_ref, s32[12]{0:T(128)S(1)} %copy-done.8, bf16[128,128]{1,0:T(8,128)(2,1)S(1)} %copy-done.4, bf16[3,7,2048]{2,1,0:T(8,128)(2,1)S(1)} %bitcast.17, bf16[12,3,16,2048]{3,2,1,0:T(8,128)(2,1)S(1)} %bitcast.13, ...), custom_call_target="tpu_custom_call" | custom-call | flops 1 | bytes 1 | tf_op jit(solution)/shard_map/pallas_call | solution.py:354
  43.7 0.0 collective-permute-done.4.rest_2_
  43.7 5.2 %collective-permute-done.5.rest_3_ = bf16[6,16,2048]{2,1,0:T(8,128)(2,1)S(1)} collective-permute-done((bf16[6,16,2048]{2,1,0:T(8,128)(2,1)S(1)}, bf16[6,16,2048]{2,1,0:T(8,128)(2,1)S(1)}, u32[]{:S(2)}, u32[]{:S(2)}) %collective-permute-start.5) | collective-permute-done | bytes 393248 | tf_op jit(solution)/shard_map/ppermute | solution.py:286
  48.9 0.0 collective-permute-done.6.rest_5_
  48.9 1.1 %collective-permute-done.7.rest_6_ = bf16[8,2048]{1,0:T(8,128)(2,1)S(1)} collective-permute-done((bf16[8,2048]{1,0:T(8,128)(2,1)S(1)}, bf16[8,2048]{1,0:T(8,128)(2,1)S(1)}, u32[]{:S(2)}, u32[]{:S(2)}) %collective-permute-start.7) | collective-permute-done | bytes 32800 | tf_op jit(solution)/shard_map/ppermute | solution.py:286
  50.0 2.5 %shard_map.118 = (bf16[12,16,2048]{2,1,0:T(8,128)(2,1)}, bf16[16,2048]{1,0:T(8,128)(2,1)}) custom-call(s32[1]{0:T(128)} %bitcast.me_ref, s32[12]{0:T(128)S(1)} %copy-done.8, s32[16]{0:T(128)S(1)} %copy-done.6, f32[12,16,2048]{2,1,0:T(8,128)S(1)} %get-tuple-element.28.query_ref, f32[12,16,2048]{2,1,0:T(8,128)S(1)} %get-tuple-element.29.conv_ref, ...), custom_call_target="tpu_custom_call" | custom-call | flops 1 | bytes 1 | tf_op jit(solution)/shard_map/pallas_call | solution.py:371
  (18 shorter events, 0.0 us)
Async XLA Ops:
  4.3 17.4 %collective-permute-start.1 = (bf16[136,2048]{1,0:T(8,128)(2,1)}, bf16[136,2048]{1,0:T(8,128)(2,1)S(1)}, u32[]{:S(2)}, u32[]{:S(2)}) collective-permute-start(bf16[136,2048]{1,0:T(8,128)(2,1)} %get-tuple-element.26), channel_id=1, source_target_pairs={{0,8},{4,12},{8,0},{12,4},{1,9},{5,13},{9,1},{13,5},{2,10},{6,14},... | collective-permute-start | bytes 1671176 | tf_op jit(solution)/shard_map/ppermute | solution.py:286
  7.3 25.3 %collective-permute-start.2 = (bf16[136,2048]{1,0:T(8,128)(2,1)}, bf16[136,2048]{1,0:T(8,128)(2,1)S(1)}, u32[]{:S(2)}, u32[]{:S(2)}) collective-permute-start(bf16[136,2048]{1,0:T(8,128)(2,1)} %get-tuple-element.27), channel_id=1, source_target_pairs={{0,12},{4,8},{8,4},{12,0},{1,13},{5,9},{9,5},{13,1},{2,14},{6,10},... | collective-permute-start | bytes 1671176 | tf_op jit(solution)/shard_map/ppermute | solution.py:286
  7.3 0.8 %copy-start.4 = (bf16[128,128]{1,0:T(8,128)(2,1)S(1)}, bf16[128,128]{1,0:T(8,128)(2,1)}, u32[]{:S(2)}) copy-start(bf16[128,128]{1,0:T(8,128)(2,1)} %filter_ref.3) | copy-start | bytes 98308
  8.1 0.7 %copy-start.5 = (s32[1,4,6]{2,1,0:T(4,128)S(1)}, s32[1,4,6]{2,1,0:T(4,128)}, u32[]{:S(2)}) copy-start(s32[1,4,6]{2,1,0:T(4,128)} %slot_ref.5) | copy-start | bytes 292
  8.8 8.5 %copy-start = (bf16[16,6,3,2048]{3,0,2,1:T(8,128)(2,1)S(1)}, bf16[16,6,3,2048]{3,0,2,1:T(8,128)(2,1)}, u32[]{:S(2)}) copy-start(bf16[16,6,3,2048]{3,0,2,1:T(8,128)(2,1)} %param.16) | copy-start | bytes 3538948
  8.8 8.5 %copy-start.2 = (bf16[16,3,2048]{2,0,1:T(8,128)(2,1)S(1)}, bf16[16,3,2048]{2,0,1:T(8,128)(2,1)}, u32[]{:S(2)}) copy-start(bf16[16,3,2048]{2,0,1:T(8,128)(2,1)} %param.13) | copy-start | bytes 589828
  8.8 8.5 %copy-start.6 = (s32[16]{0:T(128)S(1)}, s32[16]{0:T(128)}, u32[]{:S(2)}) copy-start(s32[16]{0:T(128)} %decode_owner_ref.1) | copy-start | bytes 196
  8.8 8.5 %copy-start.7 = (s32[16]{0:T(128)S(1)}, s32[16]{0:T(128)}, u32[]{:S(2)}) copy-start(s32[16]{0:T(128)} %code_ref.3) | copy-start | bytes 196
  8.8 23.8 %copy-start.3 = (bf16[7,3,2048]{2,0,1:T(8,128)(2,1)S(1)}, bf16[7,3,2048]{2,0,1:T(8,128)(2,1)}, u32[]{:S(2)}) copy-start(bf16[7,3,2048]{2,0,1:T(8,128)(2,1)} %param.18) | copy-start | bytes 258052
  19.4 13.2 %collective-permute-start = (bf16[136,2048]{1,0:T(8,128)(2,1)S(1)}, bf16[136,2048]{1,0:T(8,128)(2,1)S(1)}, u32[]{:S(2)}, u32[]{:S(2)}) collective-permute-start(bf16[136,2048]{1,0:T(8,128)(2,1)S(1)} %get-tuple-element.25), channel_id=1, source_target_pairs={{0,4},{4,0},{8,12},{12,8},{1,5},{5,1},{9,13},{13,9},{2,6},{6,2},{1... | collective-permute-start | bytes 1671176 | tf_op jit(solution)/shard_map/ppermute | solution.py:286
  19.6 17.4 %collective-permute-start.3 = (bf16[6,16,2048]{2,1,0:T(8,128)(2,1)S(1)}, bf16[6,16,2048]{2,1,0:T(8,128)(2,1)S(1)}, u32[]{:S(2)}, u32[]{:S(2)}) collective-permute-start(bf16[6,16,2048]{2,1,0:T(8,128)(2,1)S(1)} %get-tuple-element.31), channel_id=1, source_target_pairs={{0,4},{4,0},{8,12},{12,8},{1,5},{5,1},{9,13},{13,9},{2,6},{6,2},{1... | collective-permute-start | bytes 1179656 | tf_op jit(solution)/shard_map/ppermute | solution.py:286
  19.9 23.7 %collective-permute-start.4 = (bf16[6,16,2048]{2,1,0:T(8,128)(2,1)S(1)}, bf16[6,16,2048]{2,1,0:T(8,128)(2,1)S(1)}, u32[]{:S(2)}, u32[]{:S(2)}) collective-permute-start(bf16[6,16,2048]{2,1,0:T(8,128)(2,1)S(1)} %get-tuple-element.32), channel_id=1, source_target_pairs={{0,8},{4,12},{8,0},{12,4},{1,9},{5,13},{9,1},{13,5},{2,10},{6,14},... | collective-permute-start | bytes 1179656 | tf_op jit(solution)/shard_map/ppermute | solution.py:286
  21.7 27.3 %collective-permute-start.5 = (bf16[6,16,2048]{2,1,0:T(8,128)(2,1)S(1)}, bf16[6,16,2048]{2,1,0:T(8,128)(2,1)S(1)}, u32[]{:S(2)}, u32[]{:S(2)}) collective-permute-start(bf16[6,16,2048]{2,1,0:T(8,128)(2,1)S(1)} %get-tuple-element.33), channel_id=1, source_target_pairs={{0,12},{4,8},{8,4},{12,0},{1,13},{5,9},{9,5},{13,1},{2,14},{6,10},... | collective-permute-start | bytes 1179656 | tf_op jit(solution)/shard_map/ppermute | solution.py:286
  32.6 4.4 %copy-start.1 = (bf16[12,16,3,2048]{3,1,2,0:T(8,128)(2,1)S(1)}, bf16[12,16,3,2048]{3,1,2,0:T(8,128)(2,1)}, u32[]{:S(2)}) copy-start(bf16[12,16,3,2048]{3,1,2,0:T(8,128)(2,1)} %param.10) | copy-start | bytes 7077892
  32.6 4.4 %copy-start.8 = (s32[12]{0:T(128)S(1)}, s32[12]{0:T(128)}, u32[]{:S(2)}) copy-start(s32[12]{0:T(128)} %owner_ref.7) | copy-start | bytes 148
  34.7 14.2 %collective-permute-start.6 = (bf16[8,2048]{1,0:T(8,128)(2,1)S(1)}, bf16[8,2048]{1,0:T(8,128)(2,1)S(1)}, u32[]{:S(2)}, u32[]{:S(2)}) collective-permute-start(bf16[8,2048]{1,0:T(8,128)(2,1)S(1)} %get-tuple-element.37), channel_id=1, source_target_pairs={{0,4},{4,0},{8,12},{12,8},{1,5},{5,1},{9,13},{13,9},{2,6},{6,2},{1... | collective-permute-start | bytes 98312 | tf_op jit(solution)/shard_map/ppermute | solution.py:286
  34.9 15.1 %collective-permute-start.7 = (bf16[8,2048]{1,0:T(8,128)(2,1)S(1)}, bf16[8,2048]{1,0:T(8,128)(2,1)S(1)}, u32[]{:S(2)}, u32[]{:S(2)}) collective-permute-start(bf16[8,2048]{1,0:T(8,128)(2,1)S(1)} %get-tuple-element.38), channel_id=1, source_target_pairs={{0,8},{4,12},{8,0},{12,4},{1,9},{5,13},{9,1},{13,5},{2,10},{6,14},... | collective-permute-start | bytes 98312 | tf_op jit(solution)/shard_map/ppermute | solution.py:286
  37.0 13.0 %collective-permute-start.8 = (bf16[8,2048]{1,0:T(8,128)(2,1)S(1)}, bf16[8,2048]{1,0:T(8,128)(2,1)S(1)}, u32[]{:S(2)}, u32[]{:S(2)}) collective-permute-start(bf16[8,2048]{1,0:T(8,128)(2,1)S(1)} %get-tuple-element.39), channel_id=1, source_target_pairs={{0,12},{4,8},{8,4},{12,0},{1,13},{5,9},{9,5},{13,1},{2,14},{6,10},... | collective-permute-start | bytes 98312 | tf_op jit(solution)/shard_map/ppermute | solution.py:286

commit v3 on v2

--- a/solution.py
+++ b/solution.py
@@ -43,20 +43,28 @@
     return picked
 
 
-def pack_kernel(ks, cap, planes, slots, dpad, me_ref, slot_ref, owner_ref, code_ref, raw_hbm, rows_hbm, *rest):
-    outs, (raw_ref, rows_ref, raw_sel, rows_sel, sems) = rest[: len(ks)], rest[len(ks) :]
+def pack_kernel(ks, cap, planes, slots, dpad, me_ref, slot_hbm, owner_hbm, code_hbm, raw_hbm, rows_hbm, *rest):
+    outs, rest = rest[: len(ks)], rest[len(ks) :]
+    slot_ref, owner_ref, code_ref, raw_ref, rows_ref, out_ref, raw_sel, rows_sel, sems = rest
     padded = raw_sel.shape[0] // len(ks)
     decode_count = owner_ref.shape[0]
-    pairs = ((raw_hbm, raw_ref), (rows_hbm, rows_ref))
+    channels = raw_ref.shape[1]
+    piece = min(512, channels)
+    spans = [pl.ds(start, piece) for start in range(0, channels, piece)]
+    pairs = [(slot_hbm, slot_ref), (owner_hbm, owner_ref), (code_hbm, code_ref)]
+    for lanes in spans:
+        pairs += [(raw_hbm.at[:, lanes], raw_ref.at[:, lanes]), (rows_hbm.at[:, lanes], rows_ref.at[:, lanes])]
     copies = [pltpu.make_async_copy(source, target, sems.at[at]) for at, (source, target) in enumerate(pairs)]
     for copy in copies:
         copy.start()
+    for copy in copies[:3]:
+        copy.wait()
 
     row = iota((padded, 1), 0)
     column = iota((padded, planes * slots), 1)
     lane = iota((1, 3 * decode_count), 1)
     wide = iota((1, LANES), 1)
-    codes = []
+    codes, places = [], []
     for at, k in enumerate(ks):
         peer = me_ref[0] ^ k
         target = jnp.full((padded, 1), -1, jnp.int32)
@@ -75,17 +83,29 @@
                 target = jnp.where(lane == hit, rank + s * dpad, target)
             code = jnp.where(wide == jnp.where(mine, rank, -1), code_ref[n], code)
             rank += mine.astype(jnp.int32)
-        rows_sel[at] = one_hot(iota(rows_sel.shape[1:], 0), target)
+        places.append(one_hot(iota((3 * dpad, 3 * decode_count), 0), target).astype(F32))
         codes.append(code.astype(F32))
 
-    for copy in copies:
+    rows_sel[...] = jnp.concatenate(places, axis=0).astype(BF16)
+    marked = iota((padded, LANES), 0) == cap * planes
+    leaving = []
+    for step, lanes in enumerate(spans):
+        copies[3 + 2 * step].wait()
+        copies[4 + 2 * step].wait()
+        picked = dot(raw_sel[...], raw_ref[:, lanes])
+        placed = dot(rows_sel[...], rows_ref[:, lanes])
+        for at in range(len(ks)):
+            raw = picked[at * padded : (at + 1) * padded]
+            if step == 0:
+                head = jnp.where(marked, codes[at], raw[:, :LANES])
+                raw = jnp.concatenate([head, raw[:, LANES:]], axis=1)
+            rows = placed[at * 3 * dpad : (at + 1) * 3 * dpad]
+            out_ref[at, :, lanes] = jnp.concatenate([raw, rows], axis=0).astype(BF16)
+            sem = sems.at[len(copies) + len(leaving)]
+            leaving.append(pltpu.make_async_copy(out_ref.at[at, :, lanes], outs[at].at[:, lanes], sem))
+            leaving[-1].start()
+    for copy in leaving:
         copy.wait()
-    marked = iota((padded, LANES), 0) == cap * planes
-    for at in range(len(ks)):
-        raw = dot(raw_sel[at * padded : (at + 1) * padded, :], raw_ref[...])
-        head = jnp.where(marked, codes[at], raw[:, :LANES])
-        raw = jnp.concatenate([head, raw[:, LANES:]], axis=1)
-        outs[at][...] = jnp.concatenate([raw, dot(rows_sel[at], rows_ref[...])], axis=0).astype(BF16)
 
 
 def history_kernel(peers, cap, length, per_group, me_ref, slot_ref, filter_ref, hist_ref, *rest):
@@ -293,15 +313,19 @@
     def pack(ks, limit, raw_in, rows_in):
         packed = pl.pallas_call(
             functools.partial(pack_kernel, ks, cap, planes, slots, dpad),
-            in_specs=[smem] * 4 + [hbm] * 2,
-            out_specs=[vmem] * len(ks),
+            in_specs=[smem] + [hbm] * 5,
+            out_specs=[hbm] * len(ks),
             out_shape=[jax.ShapeDtypeStruct((payload, channels), BF16)] * len(ks),
             scratch_shapes=[
+                pltpu.SMEM(send_slot.shape, jnp.int32),
+                pltpu.SMEM(row_owner.shape, jnp.int32),
+                pltpu.SMEM(row_slot.shape, jnp.int32),
                 pltpu.VMEM((planes * slots, channels), BF16),
                 pltpu.VMEM((3 * decode_count, channels), BF16),
+                pltpu.VMEM((len(ks), payload, channels), BF16),
                 pltpu.VMEM((len(ks) * padded, planes * slots), BF16),
-                pltpu.VMEM((len(ks), 3 * dpad, 3 * decode_count), BF16),
-                pltpu.SemaphoreType.DMA((2,)),
+                pltpu.VMEM((len(ks) * 3 * dpad, 3 * decode_count), BF16),
+                pltpu.SemaphoreType.DMA((3 + (2 + len(ks)) * -(-channels // 512),)),
             ],
             compiler_params=pltpu.CompilerParams(vmem_limit_bytes=limit * 1024 * 1024),
             cost_estimate=cost(2 * len(ks) * padded * planes * slots * channels, 4 * planes * slots * channels),
@@ -368,17 +392,18 @@
         cost_estimate=cost(2 * count * 24 * peers * padded * channels, 14 * count * length * channels),
     )(me, stretch_owner, long_filter, weight, stretch, *sent)
 
+    wide = min(1024, channels)
     return pl.pallas_call(
         functools.partial(finish_kernel, peers, cap, dpad),
-        grid=(channels // width,),
+        grid=(channels // wide,),
         in_specs=[smem, smem, smem] + [vmem] * (2 + 2 * peers),
-        out_specs=[tiled(width, count, length), tiled(width, decode_count)],
+        out_specs=[tiled(wide, count, length), tiled(wide, decode_count)],
         out_shape=[
             jax.ShapeDtypeStruct((count, length, channels), BF16),
             jax.ShapeDtypeStruct((decode_count, channels), BF16),
         ],
         scratch_shapes=[
-            pltpu.VMEM((peers * cap, length, width), BF16),
+            pltpu.VMEM((peers * cap, length, wide), BF16),
             pltpu.SMEM((count,), jnp.int32),
             pltpu.VMEM((decode_count, peers * dpad), BF16),
         ],

time: 52.8 us -> 51.6 us (0.977)
  Pallas kernels: 25.4 us -> 24.5 us
    pallas_call x1, Pallas kernels: 2.53 us -> 1.95 us  [per_device(): pl.pallas_call(functools.partial(finish_kernel, peers, cap, dpad), grid=(...]
  transfers between devices with their start and end apart: 9 -> 9, of which waited for: 3 -> 3; matrix products, arithmetic and copies ran while one was open for 0% -> 0% of each run, Pallas kernels for 37% -> 38%
where the time goes in v3:
time: 51.6 us; the launch traced here: 51.3 us
  Pallas kernels  24.5 us (47%)
  waiting for transfers between devices  17 us (33%)
  starting transfers between devices  7.66 us (15%)
  local copies, waits for them, and re-layouts  1.47 us (3%)
  between operations  0.75 us (1%)
    ppermute x9, waiting for transfers between devices, send(): return lax.ppermute(array, 'ctx', [(i, i ^ k) for i in range(peers)])  17 us
    pallas_call x1, Pallas kernels, per_device(): pl.pallas_call(functools.partial(history_kernel, peers, cap, length, per_...  8.45 us
    ppermute x9, starting transfers between devices, send(): return lax.ppermute(array, 'ctx', [(i, i ^ k) for i in range(peers)])  7.66 us
    pallas_call x1, Pallas kernels, per_device(): pl.pallas_call(functools.partial(local_kernel, peers, planes, staps, per_...  6.65 us
    pallas_call x2, Pallas kernels, pack(): pl.pallas_call(functools.partial(pack_kernel, ks, cap, planes, slots, dpa...  5.37 us
    pallas_call x1, Pallas kernels, per_device(): pl.pallas_call(functools.partial(decode_kernel, peers, staps, slots, dpad...  2.09 us
    pallas_call x1, Pallas kernels, per_device(): pl.pallas_call(functools.partial(finish_kernel, peers, cap, dpad), grid=(...  1.95 us
    unnamed x18, local copies, waits for them, and re-layouts  1.47 us
  transfers between devices with their start and end apart: 9, of which 3 were waited for; matrix products, arithmetic and copies ran while one was open for 0% of the time, Pallas kernels for 38%

profile of v3, /device:TPU:0, one launch (start us, length us, event | category | flops | bytes accessed | tf_op | source)
XLA Modules:
  0.0 51.3 jit_solution(16402324077090830890)
XLA Ops:
  0.6 3.0 %shard_map.115 = (bf16[136,2048]{1,0:T(8,128)(2,1)}, bf16[136,2048]{1,0:T(8,128)(2,1)}) custom-call(s32[1]{0:T(128)} %bitcast.me_ref, s32[1,4,6]{2,1,0:T(4,128)} %slot_hbm.3, s32[16]{0:T(128)} %decode_owner_ref.1, s32[16]{0:T(128)} %code_hbm.3, bf16[288,2048]{1,0:T(8,128)(2,1)} %bitcast.10, bf16[48,2048]{1,0:T(8,128)(2,1)} %bitcast.14), custom_call_target="tpu_custom_call" | custom-call | flops 1 | bytes 1 | tf_op jit(solution)/shard_map/pallas_call | solution.py:314
  3.7 3.0 %collective-permute-start.1 = (bf16[136,2048]{1,0:T(8,128)(2,1)}, bf16[136,2048]{1,0:T(8,128)(2,1)S(1)}, u32[]{:S(2)}, u32[]{:S(2)}) collective-permute-start(bf16[136,2048]{1,0:T(8,128)(2,1)} %get-tuple-element.26), channel_id=1, source_target_pairs={{0,8},{4,12},{8,0},{12,4},{1,9},{5,13},{9,1},{13,5},{2,10},{6,14},... | collective-permute-start | bytes 1671176 | tf_op jit(solution)/shard_map/ppermute | solution.py:306
  6.7 0.0 collective-permute-start.2
  6.7 0.8 %copy-done.4 = bf16[128,128]{1,0:T(8,128)(2,1)S(1)} copy-done((bf16[128,128]{1,0:T(8,128)(2,1)S(1)}, bf16[128,128]{1,0:T(8,128)(2,1)}, u32[]{:S(2)}) %copy-start.4) | copy-done | bytes 32792
  7.5 0.7 %copy-done.5 = s32[1,4,6]{2,1,0:T(4,128)S(1)} copy-done((s32[1,4,6]{2,1,0:T(4,128)S(1)}, s32[1,4,6]{2,1,0:T(4,128)}, u32[]{:S(2)}) %copy-start.5) | copy-done | bytes 120
  8.2 0.0 copy-start.3
  8.2 8.5 %shard_map.113 = (bf16[6,16,2048]{2,1,0:T(8,128)(2,1)S(1)}, bf16[6,16,2048]{2,1,0:T(8,128)(2,1)S(1)}, bf16[6,16,2048]{2,1,0:T(8,128)(2,1)S(1)}, bf16[6,16,2048]{...) custom-call(s32[1]{0:T(128)} %bitcast.me_ref, s32[1,4,6]{2,1,0:T(4,128)S(1)} %copy-done.5, ...), custom_call_target="tpu_custom_call" | custom-call | flops 1 | bytes 1 | tf_op jit(solution)/shard_map/pallas_call | solution.py:339
  16.7 2.3 %shard_map.114 = (bf16[136,2048]{1,0:T(8,128)(2,1)S(1)}, bf16[136,2048]{1,0:T(8,128)(2,1)S(1)}) custom-call(s32[1]{0:T(128)} %bitcast.me_ref, s32[1,4,6]{2,1,0:T(4,128)S(1)} %copy-done.5, s32[16]{0:T(128)S(1)} %copy-done.6, s32[16]{0:T(128)S(1)} %copy-done.7, bf16[288,2048]{1,0:T(8,128)(2,1)S(1)} %bitcast.11, bf16[48,2048]{1,0:T(8,128)(2,1)S(1)} %bitcast.15), custom_call_target="tpu_custom_call" | custom-call | flops 1 | bytes 1 | tf_op jit(solution)/shard_map/pallas_call | solution.py:314
  19.0 0.3 collective-permute-start
  19.3 0.3 collective-permute-start.3
  19.6 1.7 %collective-permute-start.4 = (bf16[6,16,2048]{2,1,0:T(8,128)(2,1)S(1)}, bf16[6,16,2048]{2,1,0:T(8,128)(2,1)S(1)}, u32[]{:S(2)}, u32[]{:S(2)}) collective-permute-start(bf16[6,16,2048]{2,1,0:T(8,128)(2,1)S(1)} %get-tuple-element.32), channel_id=1, source_target_pairs={{0,8},{4,12},{8,0},{12,4},{1,9},{5,13},{9,1},{13,5},{2,10},{6,14},... | collective-permute-start | bytes 1179656 | tf_op jit(solution)/shard_map/ppermute | solution.py:306
  21.3 0.0 collective-permute-done.1.rest_2_.rest_6_
  21.3 0.1 collective-permute-start.5
  21.4 10.6 %collective-permute-done.2.rest_3_.rest_7_ = bf16[136,2048]{1,0:T(8,128)(2,1)S(1)} collective-permute-done((bf16[136,2048]{1,0:T(8,128)(2,1)}, bf16[136,2048]{1,0:T(8,128)(2,1)S(1)}, u32[]{:S(2)}, u32[]{:S(2)}) %collective-permute-start.2) | collective-permute-done | bytes 557088 | tf_op jit(solution)/shard_map/ppermute | solution.py:306
  32.0 2.1 %shard_map.117 = (bf16[8,2048]{1,0:T(8,128)(2,1)S(1)}, bf16[8,2048]{1,0:T(8,128)(2,1)S(1)}, bf16[8,2048]{1,0:T(8,128)(2,1)S(1)}, bf16[8,2048]{1,0:T(8,128)(2,1)S(1)}) custom-call(bf16[3,7,2048]{2,1,0:T(8,128)(2,1)S(1)} %bitcast.16, bf16[288,2048]{1,0:T(8,128)(2,1)S(1)} %bitcast.12, f32[16,2048]{1,0:T(8,128)S(1)} %get-tuple-element.34.first_ref, ...), custom_call_target="tpu_custom_call" | custom-call | flops 1 | bytes 1 | tf_op jit(solution)/shard_map/pallas_call | solution.py:362
  34.1 0.2 collective-permute-start.6
  34.3 2.1 %collective-permute-start.7 = (bf16[8,2048]{1,0:T(8,128)(2,1)S(1)}, bf16[8,2048]{1,0:T(8,128)(2,1)S(1)}, u32[]{:S(2)}, u32[]{:S(2)}) collective-permute-start(bf16[8,2048]{1,0:T(8,128)(2,1)S(1)} %get-tuple-element.38), channel_id=1, source_target_pairs={{0,8},{4,12},{8,0},{12,4},{1,9},{5,13},{9,1},{13,5},{2,10},{6,14},... | collective-permute-start | bytes 98312 | tf_op jit(solution)/shard_map/ppermute | solution.py:306
  36.4 0.0 collective-permute-done.3.rest_1_
  36.4 0.0 collective-permute-start.8
  36.4 6.6 %shard_map.116 = (f32[12,16,2048]{2,1,0:T(8,128)S(1)}, f32[12,16,2048]{2,1,0:T(8,128)S(1)}) custom-call(s32[1]{0:T(128)} %bitcast.me_ref, s32[12]{0:T(128)S(1)} %copy-done.8, bf16[128,128]{1,0:T(8,128)(2,1)S(1)} %copy-done.4, bf16[3,7,2048]{2,1,0:T(8,128)(2,1)S(1)} %bitcast.17, bf16[12,3,16,2048]{3,2,1,0:T(8,128)(2,1)S(1)} %bitcast.13, ...), custom_call_target="tpu_custom_call" | custom-call | flops 1 | bytes 1 | tf_op jit(solution)/shard_map/pallas_call | solution.py:378
  43.1 5.2 %collective-permute-done.5.rest_3_ = bf16[6,16,2048]{2,1,0:T(8,128)(2,1)S(1)} collective-permute-done((bf16[6,16,2048]{2,1,0:T(8,128)(2,1)S(1)}, bf16[6,16,2048]{2,1,0:T(8,128)(2,1)S(1)}, u32[]{:S(2)}, u32[]{:S(2)}) %collective-permute-start.5) | collective-permute-done | bytes 393248 | tf_op jit(solution)/shard_map/ppermute | solution.py:306
  48.3 0.0 collective-permute-done.6.rest_5_
  48.3 1.1 %collective-permute-done.7.rest_6_ = bf16[8,2048]{1,0:T(8,128)(2,1)S(1)} collective-permute-done((bf16[8,2048]{1,0:T(8,128)(2,1)S(1)}, bf16[8,2048]{1,0:T(8,128)(2,1)S(1)}, u32[]{:S(2)}, u32[]{:S(2)}) %collective-permute-start.7) | collective-permute-done | bytes 32800 | tf_op jit(solution)/shard_map/ppermute | solution.py:306
  49.4 1.9 %shard_map.118 = (bf16[12,16,2048]{2,1,0:T(8,128)(2,1)}, bf16[16,2048]{1,0:T(8,128)(2,1)}) custom-call(s32[1]{0:T(128)} %bitcast.me_ref, s32[12]{0:T(128)S(1)} %copy-done.8, s32[16]{0:T(128)S(1)} %copy-done.6, f32[12,16,2048]{2,1,0:T(8,128)S(1)} %get-tuple-element.28.query_ref, f32[12,16,2048]{2,1,0:T(8,128)S(1)} %get-tuple-element.29.conv_ref, ...), custom_call_target="tpu_custom_call" | custom-call | flops 1 | bytes 1 | tf_op jit(solution)/shard_map/pallas_call | solution.py:396
  (18 shorter events, 0.0 us)
Async XLA Ops:
  3.7 17.6 %collective-permute-start.1 = (bf16[136,2048]{1,0:T(8,128)(2,1)}, bf16[136,2048]{1,0:T(8,128)(2,1)S(1)}, u32[]{:S(2)}, u32[]{:S(2)}) collective-permute-start(bf16[136,2048]{1,0:T(8,128)(2,1)} %get-tuple-element.26), channel_id=1, source_target_pairs={{0,8},{4,12},{8,0},{12,4},{1,9},{5,13},{9,1},{13,5},{2,10},{6,14},... | collective-permute-start | bytes 1671176 | tf_op jit(solution)/shard_map/ppermute | solution.py:306
  6.7 25.3 %collective-permute-start.2 = (bf16[136,2048]{1,0:T(8,128)(2,1)}, bf16[136,2048]{1,0:T(8,128)(2,1)S(1)}, u32[]{:S(2)}, u32[]{:S(2)}) collective-permute-start(bf16[136,2048]{1,0:T(8,128)(2,1)} %get-tuple-element.27), channel_id=1, source_target_pairs={{0,12},{4,8},{8,4},{12,0},{1,13},{5,9},{9,5},{13,1},{2,14},{6,10},... | collective-permute-start | bytes 1671176 | tf_op jit(solution)/shard_map/ppermute | solution.py:306
  6.7 0.8 %copy-start.4 = (bf16[128,128]{1,0:T(8,128)(2,1)S(1)}, bf16[128,128]{1,0:T(8,128)(2,1)}, u32[]{:S(2)}) copy-start(bf16[128,128]{1,0:T(8,128)(2,1)} %filter_ref.3) | copy-start | bytes 98308
  7.5 0.7 %copy-start.5 = (s32[1,4,6]{2,1,0:T(4,128)S(1)}, s32[1,4,6]{2,1,0:T(4,128)}, u32[]{:S(2)}) copy-start(s32[1,4,6]{2,1,0:T(4,128)} %slot_hbm.3) | copy-start | bytes 292
  8.2 8.5 %copy-start = (bf16[16,6,3,2048]{3,0,2,1:T(8,128)(2,1)S(1)}, bf16[16,6,3,2048]{3,0,2,1:T(8,128)(2,1)}, u32[]{:S(2)}) copy-start(bf16[16,6,3,2048]{3,0,2,1:T(8,128)(2,1)} %param.16) | copy-start | bytes 3538948
  8.2 8.5 %copy-start.2 = (bf16[16,3,2048]{2,0,1:T(8,128)(2,1)S(1)}, bf16[16,3,2048]{2,0,1:T(8,128)(2,1)}, u32[]{:S(2)}) copy-start(bf16[16,3,2048]{2,0,1:T(8,128)(2,1)} %param.13) | copy-start | bytes 589828
  8.2 8.5 %copy-start.6 = (s32[16]{0:T(128)S(1)}, s32[16]{0:T(128)}, u32[]{:S(2)}) copy-start(s32[16]{0:T(128)} %decode_owner_ref.1) | copy-start | bytes 196
  8.2 8.5 %copy-start.7 = (s32[16]{0:T(128)S(1)}, s32[16]{0:T(128)}, u32[]{:S(2)}) copy-start(s32[16]{0:T(128)} %code_hbm.3) | copy-start | bytes 196
  8.2 23.8 %copy-start.3 = (bf16[7,3,2048]{2,0,1:T(8,128)(2,1)S(1)}, bf16[7,3,2048]{2,0,1:T(8,128)(2,1)}, u32[]{:S(2)}) copy-start(bf16[7,3,2048]{2,0,1:T(8,128)(2,1)} %param.18) | copy-start | bytes 258052
  19.0 13.0 %collective-permute-start = (bf16[136,2048]{1,0:T(8,128)(2,1)S(1)}, bf16[136,2048]{1,0:T(8,128)(2,1)S(1)}, u32[]{:S(2)}, u32[]{:S(2)}) collective-permute-start(bf16[136,2048]{1,0:T(8,128)(2,1)S(1)} %get-tuple-element.25), channel_id=1, source_target_pairs={{0,4},{4,0},{8,12},{12,8},{1,5},{5,1},{9,13},{13,9},{2,6},{6,2},{1... | collective-permute-start | bytes 1671176 | tf_op jit(solution)/shard_map/ppermute | solution.py:306
  19.3 17.1 %collective-permute-start.3 = (bf16[6,16,2048]{2,1,0:T(8,128)(2,1)S(1)}, bf16[6,16,2048]{2,1,0:T(8,128)(2,1)S(1)}, u32[]{:S(2)}, u32[]{:S(2)}) collective-permute-start(bf16[6,16,2048]{2,1,0:T(8,128)(2,1)S(1)} %get-tuple-element.31), channel_id=1, source_target_pairs={{0,4},{4,0},{8,12},{12,8},{1,5},{5,1},{9,13},{13,9},{2,6},{6,2},{1... | collective-permute-start | bytes 1179656 | tf_op jit(solution)/shard_map/ppermute | solution.py:306
  19.6 23.5 %collective-permute-start.4 = (bf16[6,16,2048]{2,1,0:T(8,128)(2,1)S(1)}, bf16[6,16,2048]{2,1,0:T(8,128)(2,1)S(1)}, u32[]{:S(2)}, u32[]{:S(2)}) collective-permute-start(bf16[6,16,2048]{2,1,0:T(8,128)(2,1)S(1)} %get-tuple-element.32), channel_id=1, source_target_pairs={{0,8},{4,12},{8,0},{12,4},{1,9},{5,13},{9,1},{13,5},{2,10},{6,14},... | collective-permute-start | bytes 1179656 | tf_op jit(solution)/shard_map/ppermute | solution.py:306
  21.3 27.0 %collective-permute-start.5 = (bf16[6,16,2048]{2,1,0:T(8,128)(2,1)S(1)}, bf16[6,16,2048]{2,1,0:T(8,128)(2,1)S(1)}, u32[]{:S(2)}, u32[]{:S(2)}) collective-permute-start(bf16[6,16,2048]{2,1,0:T(8,128)(2,1)S(1)} %get-tuple-element.33), channel_id=1, source_target_pairs={{0,12},{4,8},{8,4},{12,0},{1,13},{5,9},{9,5},{13,1},{2,14},{6,10},... | collective-permute-start | bytes 1179656 | tf_op jit(solution)/shard_map/ppermute | solution.py:306
  32.0 4.4 %copy-start.1 = (bf16[12,16,3,2048]{3,1,2,0:T(8,128)(2,1)S(1)}, bf16[12,16,3,2048]{3,1,2,0:T(8,128)(2,1)}, u32[]{:S(2)}) copy-start(bf16[12,16,3,2048]{3,1,2,0:T(8,128)(2,1)} %param.10) | copy-start | bytes 7077892
  32.0 4.4 %copy-start.8 = (s32[12]{0:T(128)S(1)}, s32[12]{0:T(128)}, u32[]{:S(2)}) copy-start(s32[12]{0:T(128)} %owner_ref.3) | copy-start | bytes 148
  34.1 14.2 %collective-permute-start.6 = (bf16[8,2048]{1,0:T(8,128)(2,1)S(1)}, bf16[8,2048]{1,0:T(8,128)(2,1)S(1)}, u32[]{:S(2)}, u32[]{:S(2)}) collective-permute-start(bf16[8,2048]{1,0:T(8,128)(2,1)S(1)} %get-tuple-element.37), channel_id=1, source_target_pairs={{0,4},{4,0},{8,12},{12,8},{1,5},{5,1},{9,13},{13,9},{2,6},{6,2},{1... | collective-permute-start | bytes 98312 | tf_op jit(solution)/shard_map/ppermute | solution.py:306
  34.3 15.1 %collective-permute-start.7 = (bf16[8,2048]{1,0:T(8,128)(2,1)S(1)}, bf16[8,2048]{1,0:T(8,128)(2,1)S(1)}, u32[]{:S(2)}, u32[]{:S(2)}) collective-permute-start(bf16[8,2048]{1,0:T(8,128)(2,1)S(1)} %get-tuple-element.38), channel_id=1, source_target_pairs={{0,8},{4,12},{8,0},{12,4},{1,9},{5,13},{9,1},{13,5},{2,10},{6,14},... | collective-permute-start | bytes 98312 | tf_op jit(solution)/shard_map/ppermute | solution.py:306
  36.4 13.0 %collective-permute-start.8 = (bf16[8,2048]{1,0:T(8,128)(2,1)S(1)}, bf16[8,2048]{1,0:T(8,128)(2,1)S(1)}, u32[]{:S(2)}, u32[]{:S(2)}) collective-permute-start(bf16[8,2048]{1,0:T(8,128)(2,1)S(1)} %get-tuple-element.39), channel_id=1, source_target_pairs={{0,12},{4,8},{8,4},{12,0},{1,13},{5,9},{9,5},{13,1},{2,14},{6,10},... | collective-permute-start | bytes 98312 | tf_op jit(solution)/shard_map/ppermute | solution.py:306

commit v4 on v3

--- a/solution.py
+++ b/solution.py
@@ -291,7 +291,7 @@
     smem = pl.BlockSpec(memory_space=pltpu.SMEM)
     vmem = pl.BlockSpec(memory_space=pltpu.VMEM)
     hbm = pl.BlockSpec(memory_space=pltpu.HBM)
-    params = pltpu.CompilerParams(vmem_limit_bytes=32 * 1024 * 1024)
+    params = pltpu.CompilerParams(vmem_limit_bytes=24 * 1024 * 1024)
 
     def tiled(width, *lead):
         return pl.BlockSpec((*lead, width), lambda t: (0,) * len(lead) + (t,))

time: 51.6 us -> 51.6 us (level)
  no operation moved by 1% of the time
where the time goes in v4:
time: 51.6 us; the launch traced here: 51.3 us
  Pallas kernels  24.5 us (47%)
  waiting for transfers between devices  16.9 us (33%)
  starting transfers between devices  7.66 us (15%)
  local copies, waits for them, and re-layouts  1.47 us (3%)
  between operations  0.75 us (1%)
    ppermute x9, waiting for transfers between devices, send(): return lax.ppermute(array, 'ctx', [(i, i ^ k) for i in range(peers)])  16.9 us
    pallas_call x1, Pallas kernels, per_device(): pl.pallas_call(functools.partial(history_kernel, peers, cap, length, per_...  8.45 us
    ppermute x9, starting transfers between devices, send(): return lax.ppermute(array, 'ctx', [(i, i ^ k) for i in range(peers)])  7.66 us
    pallas_call x1, Pallas kernels, per_device(): pl.pallas_call(functools.partial(local_kernel, peers, planes, staps, per_...  6.65 us
    pallas_call x2, Pallas kernels, pack(): pl.pallas_call(functools.partial(pack_kernel, ks, cap, planes, slots, dpa...  5.38 us
    pallas_call x1, Pallas kernels, per_device(): pl.pallas_call(functools.partial(decode_kernel, peers, staps, slots, dpad...  2.09 us
    pallas_call x1, Pallas kernels, per_device(): pl.pallas_call(functools.partial(finish_kernel, peers, cap, dpad), grid=(...  1.95 us
    unnamed x18, local copies, waits for them, and re-layouts  1.47 us
  transfers between devices with their start and end apart: 9, of which 3 were waited for; matrix products, arithmetic and copies ran while one was open for 0% of the time, Pallas kernels for 38%

profile of v4, /device:TPU:0, one launch (start us, length us, event | category | flops | bytes accessed | tf_op | source)
XLA Modules:
  0.0 51.3 jit_solution(2115485894759718296)
XLA Ops:
  0.6 3.0 %shard_map.115 = (bf16[136,2048]{1,0:T(8,128)(2,1)}, bf16[136,2048]{1,0:T(8,128)(2,1)}) custom-call(s32[1]{0:T(128)} %bitcast.me_ref, s32[1,4,6]{2,1,0:T(4,128)} %slot_hbm.3, s32[16]{0:T(128)} %decode_owner_ref.1, s32[16]{0:T(128)} %code_hbm.3, bf16[288,2048]{1,0:T(8,128)(2,1)} %bitcast.10, bf16[48,2048]{1,0:T(8,128)(2,1)} %bitcast.14), custom_call_target="tpu_custom_call" | custom-call | flops 1 | bytes 1 | tf_op jit(solution)/shard_map/pallas_call | solution.py:314
  3.7 3.0 %collective-permute-start.1 = (bf16[136,2048]{1,0:T(8,128)(2,1)}, bf16[136,2048]{1,0:T(8,128)(2,1)S(1)}, u32[]{:S(2)}, u32[]{:S(2)}) collective-permute-start(bf16[136,2048]{1,0:T(8,128)(2,1)} %get-tuple-element.26), channel_id=1, source_target_pairs={{0,8},{4,12},{8,0},{12,4},{1,9},{5,13},{9,1},{13,5},{2,10},{6,14},... | collective-permute-start | bytes 1671176 | tf_op jit(solution)/shard_map/ppermute | solution.py:306
  6.7 0.0 collective-permute-start.2
  6.7 0.8 %copy-done.4 = bf16[128,128]{1,0:T(8,128)(2,1)S(1)} copy-done((bf16[128,128]{1,0:T(8,128)(2,1)S(1)}, bf16[128,128]{1,0:T(8,128)(2,1)}, u32[]{:S(2)}) %copy-start.4) | copy-done | bytes 32792
  7.5 0.7 %copy-done.5 = s32[1,4,6]{2,1,0:T(4,128)S(1)} copy-done((s32[1,4,6]{2,1,0:T(4,128)S(1)}, s32[1,4,6]{2,1,0:T(4,128)}, u32[]{:S(2)}) %copy-start.5) | copy-done | bytes 120
  8.2 0.0 copy-start.3
  8.2 8.5 %shard_map.113 = (bf16[6,16,2048]{2,1,0:T(8,128)(2,1)S(1)}, bf16[6,16,2048]{2,1,0:T(8,128)(2,1)S(1)}, bf16[6,16,2048]{2,1,0:T(8,128)(2,1)S(1)}, bf16[6,16,2048]{...) custom-call(s32[1]{0:T(128)} %bitcast.me_ref, s32[1,4,6]{2,1,0:T(4,128)S(1)} %copy-done.5, ...), custom_call_target="tpu_custom_call" | custom-call | flops 1 | bytes 1 | tf_op jit(solution)/shard_map/pallas_call | solution.py:339
  16.7 2.3 %shard_map.114 = (bf16[136,2048]{1,0:T(8,128)(2,1)S(1)}, bf16[136,2048]{1,0:T(8,128)(2,1)S(1)}) custom-call(s32[1]{0:T(128)} %bitcast.me_ref, s32[1,4,6]{2,1,0:T(4,128)S(1)} %copy-done.5, s32[16]{0:T(128)S(1)} %copy-done.6, s32[16]{0:T(128)S(1)} %copy-done.7, bf16[288,2048]{1,0:T(8,128)(2,1)S(1)} %bitcast.11, bf16[48,2048]{1,0:T(8,128)(2,1)S(1)} %bitcast.15), custom_call_target="tpu_custom_call" | custom-call | flops 1 | bytes 1 | tf_op jit(solution)/shard_map/pallas_call | solution.py:314
  19.0 0.3 collective-permute-start
  19.3 0.3 collective-permute-start.3
  19.6 1.7 %collective-permute-start.4 = (bf16[6,16,2048]{2,1,0:T(8,128)(2,1)S(1)}, bf16[6,16,2048]{2,1,0:T(8,128)(2,1)S(1)}, u32[]{:S(2)}, u32[]{:S(2)}) collective-permute-start(bf16[6,16,2048]{2,1,0:T(8,128)(2,1)S(1)} %get-tuple-element.32), channel_id=1, source_target_pairs={{0,8},{4,12},{8,0},{12,4},{1,9},{5,13},{9,1},{13,5},{2,10},{6,14},... | collective-permute-start | bytes 1179656 | tf_op jit(solution)/shard_map/ppermute | solution.py:306
  21.3 0.0 collective-permute-done.1.rest_2_.rest_6_
  21.3 0.1 collective-permute-start.5
  21.4 10.6 %collective-permute-done.2.rest_3_.rest_7_ = bf16[136,2048]{1,0:T(8,128)(2,1)S(1)} collective-permute-done((bf16[136,2048]{1,0:T(8,128)(2,1)}, bf16[136,2048]{1,0:T(8,128)(2,1)S(1)}, u32[]{:S(2)}, u32[]{:S(2)}) %collective-permute-start.2) | collective-permute-done | bytes 557088 | tf_op jit(solution)/shard_map/ppermute | solution.py:306
  32.0 2.1 %shard_map.117 = (bf16[8,2048]{1,0:T(8,128)(2,1)S(1)}, bf16[8,2048]{1,0:T(8,128)(2,1)S(1)}, bf16[8,2048]{1,0:T(8,128)(2,1)S(1)}, bf16[8,2048]{1,0:T(8,128)(2,1)S(1)}) custom-call(bf16[3,7,2048]{2,1,0:T(8,128)(2,1)S(1)} %bitcast.16, bf16[288,2048]{1,0:T(8,128)(2,1)S(1)} %bitcast.12, f32[16,2048]{1,0:T(8,128)S(1)} %get-tuple-element.34.first_ref, ...), custom_call_target="tpu_custom_call" | custom-call | flops 1 | bytes 1 | tf_op jit(solution)/shard_map/pallas_call | solution.py:362
  34.1 0.2 collective-permute-start.6
  34.3 2.1 %collective-permute-start.7 = (bf16[8,2048]{1,0:T(8,128)(2,1)S(1)}, bf16[8,2048]{1,0:T(8,128)(2,1)S(1)}, u32[]{:S(2)}, u32[]{:S(2)}) collective-permute-start(bf16[8,2048]{1,0:T(8,128)(2,1)S(1)} %get-tuple-element.38), channel_id=1, source_target_pairs={{0,8},{4,12},{8,0},{12,4},{1,9},{5,13},{9,1},{13,5},{2,10},{6,14},... | collective-permute-start | bytes 98312 | tf_op jit(solution)/shard_map/ppermute | solution.py:306
  36.4 0.0 collective-permute-done.3.rest_1_
  36.4 0.0 collective-permute-start.8
  36.4 6.6 %shard_map.116 = (f32[12,16,2048]{2,1,0:T(8,128)S(1)}, f32[12,16,2048]{2,1,0:T(8,128)S(1)}) custom-call(s32[1]{0:T(128)} %bitcast.me_ref, s32[12]{0:T(128)S(1)} %copy-done.8, bf16[128,128]{1,0:T(8,128)(2,1)S(1)} %copy-done.4, bf16[3,7,2048]{2,1,0:T(8,128)(2,1)S(1)} %bitcast.17, bf16[12,3,16,2048]{3,2,1,0:T(8,128)(2,1)S(1)} %bitcast.13, ...), custom_call_target="tpu_custom_call" | custom-call | flops 1 | bytes 1 | tf_op jit(solution)/shard_map/pallas_call | solution.py:378
  43.1 5.2 %collective-permute-done.5.rest_3_ = bf16[6,16,2048]{2,1,0:T(8,128)(2,1)S(1)} collective-permute-done((bf16[6,16,2048]{2,1,0:T(8,128)(2,1)S(1)}, bf16[6,16,2048]{2,1,0:T(8,128)(2,1)S(1)}, u32[]{:S(2)}, u32[]{:S(2)}) %collective-permute-start.5) | collective-permute-done | bytes 393248 | tf_op jit(solution)/shard_map/ppermute | solution.py:306
  48.3 0.0 collective-permute-done.6.rest_5_
  48.3 1.1 %collective-permute-done.7.rest_6_ = bf16[8,2048]{1,0:T(8,128)(2,1)S(1)} collective-permute-done((bf16[8,2048]{1,0:T(8,128)(2,1)S(1)}, bf16[8,2048]{1,0:T(8,128)(2,1)S(1)}, u32[]{:S(2)}, u32[]{:S(2)}) %collective-permute-start.7) | collective-permute-done | bytes 32800 | tf_op jit(solution)/shard_map/ppermute | solution.py:306
  49.4 1.9 %shard_map.118 = (bf16[12,16,2048]{2,1,0:T(8,128)(2,1)}, bf16[16,2048]{1,0:T(8,128)(2,1)}) custom-call(s32[1]{0:T(128)} %bitcast.me_ref, s32[12]{0:T(128)S(1)} %copy-done.8, s32[16]{0:T(128)S(1)} %copy-done.6, f32[12,16,2048]{2,1,0:T(8,128)S(1)} %get-tuple-element.28.query_ref, f32[12,16,2048]{2,1,0:T(8,128)S(1)} %get-tuple-element.29.conv_ref, ...), custom_call_target="tpu_custom_call" | custom-call | flops 1 | bytes 1 | tf_op jit(solution)/shard_map/pallas_call | solution.py:396
  (18 shorter events, 0.0 us)
Async XLA Ops:
  3.7 17.6 %collective-permute-start.1 = (bf16[136,2048]{1,0:T(8,128)(2,1)}, bf16[136,2048]{1,0:T(8,128)(2,1)S(1)}, u32[]{:S(2)}, u32[]{:S(2)}) collective-permute-start(bf16[136,2048]{1,0:T(8,128)(2,1)} %get-tuple-element.26), channel_id=1, source_target_pairs={{0,8},{4,12},{8,0},{12,4},{1,9},{5,13},{9,1},{13,5},{2,10},{6,14},... | collective-permute-start | bytes 1671176 | tf_op jit(solution)/shard_map/ppermute | solution.py:306
  6.7 25.3 %collective-permute-start.2 = (bf16[136,2048]{1,0:T(8,128)(2,1)}, bf16[136,2048]{1,0:T(8,128)(2,1)S(1)}, u32[]{:S(2)}, u32[]{:S(2)}) collective-permute-start(bf16[136,2048]{1,0:T(8,128)(2,1)} %get-tuple-element.27), channel_id=1, source_target_pairs={{0,12},{4,8},{8,4},{12,0},{1,13},{5,9},{9,5},{13,1},{2,14},{6,10},... | collective-permute-start | bytes 1671176 | tf_op jit(solution)/shard_map/ppermute | solution.py:306
  6.7 0.8 %copy-start.4 = (bf16[128,128]{1,0:T(8,128)(2,1)S(1)}, bf16[128,128]{1,0:T(8,128)(2,1)}, u32[]{:S(2)}) copy-start(bf16[128,128]{1,0:T(8,128)(2,1)} %filter_ref.3) | copy-start | bytes 98308
  7.5 0.7 %copy-start.5 = (s32[1,4,6]{2,1,0:T(4,128)S(1)}, s32[1,4,6]{2,1,0:T(4,128)}, u32[]{:S(2)}) copy-start(s32[1,4,6]{2,1,0:T(4,128)} %slot_hbm.3) | copy-start | bytes 292
  8.2 8.5 %copy-start = (bf16[16,6,3,2048]{3,0,2,1:T(8,128)(2,1)S(1)}, bf16[16,6,3,2048]{3,0,2,1:T(8,128)(2,1)}, u32[]{:S(2)}) copy-start(bf16[16,6,3,2048]{3,0,2,1:T(8,128)(2,1)} %param.16) | copy-start | bytes 3538948
  8.2 8.5 %copy-start.2 = (bf16[16,3,2048]{2,0,1:T(8,128)(2,1)S(1)}, bf16[16,3,2048]{2,0,1:T(8,128)(2,1)}, u32[]{:S(2)}) copy-start(bf16[16,3,2048]{2,0,1:T(8,128)(2,1)} %param.13) | copy-start | bytes 589828
  8.2 8.5 %copy-start.6 = (s32[16]{0:T(128)S(1)}, s32[16]{0:T(128)}, u32[]{:S(2)}) copy-start(s32[16]{0:T(128)} %decode_owner_ref.1) | copy-start | bytes 196
  8.2 8.5 %copy-start.7 = (s32[16]{0:T(128)S(1)}, s32[16]{0:T(128)}, u32[]{:S(2)}) copy-start(s32[16]{0:T(128)} %code_hbm.3) | copy-start | bytes 196
  8.2 23.8 %copy-start.3 = (bf16[7,3,2048]{2,0,1:T(8,128)(2,1)S(1)}, bf16[7,3,2048]{2,0,1:T(8,128)(2,1)}, u32[]{:S(2)}) copy-start(bf16[7,3,2048]{2,0,1:T(8,128)(2,1)} %param.18) | copy-start | bytes 258052
  19.0 13.0 %collective-permute-start = (bf16[136,2048]{1,0:T(8,128)(2,1)S(1)}, bf16[136,2048]{1,0:T(8,128)(2,1)S(1)}, u32[]{:S(2)}, u32[]{:S(2)}) collective-permute-start(bf16[136,2048]{1,0:T(8,128)(2,1)S(1)} %get-tuple-element.25), channel_id=1, source_target_pairs={{0,4},{4,0},{8,12},{12,8},{1,5},{5,1},{9,13},{13,9},{2,6},{6,2},{1... | collective-permute-start | bytes 1671176 | tf_op jit(solution)/shard_map/ppermute | solution.py:306
  19.3 17.1 %collective-permute-start.3 = (bf16[6,16,2048]{2,1,0:T(8,128)(2,1)S(1)}, bf16[6,16,2048]{2,1,0:T(8,128)(2,1)S(1)}, u32[]{:S(2)}, u32[]{:S(2)}) collective-permute-start(bf16[6,16,2048]{2,1,0:T(8,128)(2,1)S(1)} %get-tuple-element.31), channel_id=1, source_target_pairs={{0,4},{4,0},{8,12},{12,8},{1,5},{5,1},{9,13},{13,9},{2,6},{6,2},{1... | collective-permute-start | bytes 1179656 | tf_op jit(solution)/shard_map/ppermute | solution.py:306
  19.6 23.5 %collective-permute-start.4 = (bf16[6,16,2048]{2,1,0:T(8,128)(2,1)S(1)}, bf16[6,16,2048]{2,1,0:T(8,128)(2,1)S(1)}, u32[]{:S(2)}, u32[]{:S(2)}) collective-permute-start(bf16[6,16,2048]{2,1,0:T(8,128)(2,1)S(1)} %get-tuple-element.32), channel_id=1, source_target_pairs={{0,8},{4,12},{8,0},{12,4},{1,9},{5,13},{9,1},{13,5},{2,10},{6,14},... | collective-permute-start | bytes 1179656 | tf_op jit(solution)/shard_map/ppermute | solution.py:306
  21.3 27.0 %collective-permute-start.5 = (bf16[6,16,2048]{2,1,0:T(8,128)(2,1)S(1)}, bf16[6,16,2048]{2,1,0:T(8,128)(2,1)S(1)}, u32[]{:S(2)}, u32[]{:S(2)}) collective-permute-start(bf16[6,16,2048]{2,1,0:T(8,128)(2,1)S(1)} %get-tuple-element.33), channel_id=1, source_target_pairs={{0,12},{4,8},{8,4},{12,0},{1,13},{5,9},{9,5},{13,1},{2,14},{6,10},... | collective-permute-start | bytes 1179656 | tf_op jit(solution)/shard_map/ppermute | solution.py:306
  32.0 4.4 %copy-start.1 = (bf16[12,16,3,2048]{3,1,2,0:T(8,128)(2,1)S(1)}, bf16[12,16,3,2048]{3,1,2,0:T(8,128)(2,1)}, u32[]{:S(2)}) copy-start(bf16[12,16,3,2048]{3,1,2,0:T(8,128)(2,1)} %param.10) | copy-start | bytes 7077892
  32.0 4.4 %copy-start.8 = (s32[12]{0:T(128)S(1)}, s32[12]{0:T(128)}, u32[]{:S(2)}) copy-start(s32[12]{0:T(128)} %owner_ref.3) | copy-start | bytes 148
  34.1 14.2 %collective-permute-start.6 = (bf16[8,2048]{1,0:T(8,128)(2,1)S(1)}, bf16[8,2048]{1,0:T(8,128)(2,1)S(1)}, u32[]{:S(2)}, u32[]{:S(2)}) collective-permute-start(bf16[8,2048]{1,0:T(8,128)(2,1)S(1)} %get-tuple-element.37), channel_id=1, source_target_pairs={{0,4},{4,0},{8,12},{12,8},{1,5},{5,1},{9,13},{13,9},{2,6},{6,2},{1... | collective-permute-start | bytes 98312 | tf_op jit(solution)/shard_map/ppermute | solution.py:306
  34.3 15.1 %collective-permute-start.7 = (bf16[8,2048]{1,0:T(8,128)(2,1)S(1)}, bf16[8,2048]{1,0:T(8,128)(2,1)S(1)}, u32[]{:S(2)}, u32[]{:S(2)}) collective-permute-start(bf16[8,2048]{1,0:T(8,128)(2,1)S(1)} %get-tuple-element.38), channel_id=1, source_target_pairs={{0,8},{4,12},{8,0},{12,4},{1,9},{5,13},{9,1},{13,5},{2,10},{6,14},... | collective-permute-start | bytes 98312 | tf_op jit(solution)/shard_map/ppermute | solution.py:306
  36.4 13.0 %collective-permute-start.8 = (bf16[8,2048]{1,0:T(8,128)(2,1)S(1)}, bf16[8,2048]{1,0:T(8,128)(2,1)S(1)}, u32[]{:S(2)}, u32[]{:S(2)}) collective-permute-start(bf16[8,2048]{1,0:T(8,128)(2,1)S(1)} %get-tuple-element.39), channel_id=1, source_target_pairs={{0,12},{4,8},{8,4},{12,0},{1,13},{5,9},{9,5},{13,1},{2,14},{6,10},... | collective-permute-start | bytes 98312 | tf_op jit(solution)/shard_map/ppermute | solution.py:306

commit v5 on v4

--- a/solution.py
+++ b/solution.py
@@ -49,7 +49,7 @@
     padded = raw_sel.shape[0] // len(ks)
     decode_count = owner_ref.shape[0]
     channels = raw_ref.shape[1]
-    piece = min(512, channels)
+    piece = min(1024, channels)
     spans = [pl.ds(start, piece) for start in range(0, channels, piece)]
     pairs = [(slot_hbm, slot_ref), (owner_hbm, owner_ref), (code_hbm, code_ref)]
     for lanes in spans:
@@ -325,7 +325,7 @@
                 pltpu.VMEM((len(ks), payload, channels), BF16),
                 pltpu.VMEM((len(ks) * padded, planes * slots), BF16),
                 pltpu.VMEM((len(ks) * 3 * dpad, 3 * decode_count), BF16),
-                pltpu.SemaphoreType.DMA((3 + (2 + len(ks)) * -(-channels // 512),)),
+                pltpu.SemaphoreType.DMA((3 + (2 + len(ks)) * -(-channels // 1024),)),
             ],
             compiler_params=pltpu.CompilerParams(vmem_limit_bytes=limit * 1024 * 1024),
             cost_estimate=cost(2 * len(ks) * padded * planes * slots * channels, 4 * planes * slots * channels),

time: 51.6 us -> 51.4 us (level)
  Pallas kernels: 24.5 us -> 23.8 us
    pallas_call x2, Pallas kernels: 5.38 us -> 4.66 us  [pack(): pl.pallas_call(functools.partial(pack_kernel, ks, cap, planes, slots, dpa...]
  transfers between devices with their start and end apart: 9 -> 9, of which waited for: 3 -> 3; matrix products, arithmetic and copies ran while one was open for 0% -> 0% of each run, Pallas kernels for 38% -> 37%
where the time goes in v5:
time: 51.4 us; the launch traced here: 51.1 us
  Pallas kernels  23.8 us (46%)
  waiting for transfers between devices  17.4 us (34%)
  starting transfers between devices  7.67 us (15%)
  local copies, waits for them, and re-layouts  1.47 us (3%)
  between operations  0.75 us (1%)
    ppermute x9, waiting for transfers between devices, send(): return lax.ppermute(array, 'ctx', [(i, i ^ k) for i in range(peers)])  17.4 us
    pallas_call x1, Pallas kernels, per_device(): pl.pallas_call(functools.partial(history_kernel, peers, cap, length, per_...  8.45 us
    ppermute x9, starting transfers between devices, send(): return lax.ppermute(array, 'ctx', [(i, i ^ k) for i in range(peers)])  7.67 us
    pallas_call x1, Pallas kernels, per_device(): pl.pallas_call(functools.partial(local_kernel, peers, planes, staps, per_...  6.65 us
    pallas_call x2, Pallas kernels, pack(): pl.pallas_call(functools.partial(pack_kernel, ks, cap, planes, slots, dpa...  4.66 us
    pallas_call x1, Pallas kernels, per_device(): pl.pallas_call(functools.partial(decode_kernel, peers, staps, slots, dpad...  2.1 us
    pallas_call x1, Pallas kernels, per_device(): pl.pallas_call(functools.partial(finish_kernel, peers, cap, dpad), grid=(...  1.95 us
    unnamed x18, local copies, waits for them, and re-layouts  1.47 us
  transfers between devices with their start and end apart: 9, of which 3 were waited for; matrix products, arithmetic and copies ran while one was open for 0% of the time, Pallas kernels for 37%

profile of v5, /device:TPU:0, one launch (start us, length us, event | category | flops | bytes accessed | tf_op | source)
XLA Modules:
  0.0 51.1 jit_solution(16401480374870634963)
XLA Ops:
  0.6 2.8 %shard_map.115 = (bf16[136,2048]{1,0:T(8,128)(2,1)}, bf16[136,2048]{1,0:T(8,128)(2,1)}) custom-call(s32[1]{0:T(128)} %bitcast.me_ref, s32[1,4,6]{2,1,0:T(4,128)} %slot_hbm.3, s32[16]{0:T(128)} %decode_owner_ref.1, s32[16]{0:T(128)} %code_hbm.3, bf16[288,2048]{1,0:T(8,128)(2,1)} %bitcast.10, bf16[48,2048]{1,0:T(8,128)(2,1)} %bitcast.14), custom_call_target="tpu_custom_call" | custom-call | flops 1 | bytes 1 | tf_op jit(solution)/shard_map/pallas_call | solution.py:314
  3.5 3.0 %collective-permute-start.1 = (bf16[136,2048]{1,0:T(8,128)(2,1)}, bf16[136,2048]{1,0:T(8,128)(2,1)S(1)}, u32[]{:S(2)}, u32[]{:S(2)}) collective-permute-start(bf16[136,2048]{1,0:T(8,128)(2,1)} %get-tuple-element.26), channel_id=1, source_target_pairs={{0,8},{4,12},{8,0},{12,4},{1,9},{5,13},{9,1},{13,5},{2,10},{6,14},... | collective-permute-start | bytes 1671176 | tf_op jit(solution)/shard_map/ppermute | solution.py:306
  6.5 0.0 collective-permute-start.2
  6.5 0.8 %copy-done.4 = bf16[128,128]{1,0:T(8,128)(2,1)S(1)} copy-done((bf16[128,128]{1,0:T(8,128)(2,1)S(1)}, bf16[128,128]{1,0:T(8,128)(2,1)}, u32[]{:S(2)}) %copy-start.4) | copy-done | bytes 32792
  7.3 0.7 %copy-done.5 = s32[1,4,6]{2,1,0:T(4,128)S(1)} copy-done((s32[1,4,6]{2,1,0:T(4,128)S(1)}, s32[1,4,6]{2,1,0:T(4,128)}, u32[]{:S(2)}) %copy-start.5) | copy-done | bytes 120
  8.0 0.0 copy-start.3
  8.0 8.4 %shard_map.113 = (bf16[6,16,2048]{2,1,0:T(8,128)(2,1)S(1)}, bf16[6,16,2048]{2,1,0:T(8,128)(2,1)S(1)}, bf16[6,16,2048]{2,1,0:T(8,128)(2,1)S(1)}, bf16[6,16,2048]{...) custom-call(s32[1]{0:T(128)} %bitcast.me_ref, s32[1,4,6]{2,1,0:T(4,128)S(1)} %copy-done.5, ...), custom_call_target="tpu_custom_call" | custom-call | flops 1 | bytes 1 | tf_op jit(solution)/shard_map/pallas_call | solution.py:339
  16.5 1.8 %shard_map.114 = (bf16[136,2048]{1,0:T(8,128)(2,1)S(1)}, bf16[136,2048]{1,0:T(8,128)(2,1)S(1)}) custom-call(s32[1]{0:T(128)} %bitcast.me_ref, s32[1,4,6]{2,1,0:T(4,128)S(1)} %copy-done.5, s32[16]{0:T(128)S(1)} %copy-done.6, s32[16]{0:T(128)S(1)} %copy-done.7, bf16[288,2048]{1,0:T(8,128)(2,1)S(1)} %bitcast.11, bf16[48,2048]{1,0:T(8,128)(2,1)S(1)} %bitcast.15), custom_call_target="tpu_custom_call" | custom-call | flops 1 | bytes 1 | tf_op jit(solution)/shard_map/pallas_call | solution.py:314
  18.3 0.3 collective-permute-start
  18.6 0.3 collective-permute-start.3
  18.9 1.7 %collective-permute-start.4 = (bf16[6,16,2048]{2,1,0:T(8,128)(2,1)S(1)}, bf16[6,16,2048]{2,1,0:T(8,128)(2,1)S(1)}, u32[]{:S(2)}, u32[]{:S(2)}) collective-permute-start(bf16[6,16,2048]{2,1,0:T(8,128)(2,1)S(1)} %get-tuple-element.32), channel_id=1, source_target_pairs={{0,8},{4,12},{8,0},{12,4},{1,9},{5,13},{9,1},{13,5},{2,10},{6,14},... | collective-permute-start | bytes 1179656 | tf_op jit(solution)/shard_map/ppermute | solution.py:306
  20.6 0.0 collective-permute-done.1.rest_2_.rest_6_
  20.6 0.1 collective-permute-start.5
  20.7 11.1 %collective-permute-done.2.rest_3_.rest_7_ = bf16[136,2048]{1,0:T(8,128)(2,1)S(1)} collective-permute-done((bf16[136,2048]{1,0:T(8,128)(2,1)}, bf16[136,2048]{1,0:T(8,128)(2,1)S(1)}, u32[]{:S(2)}, u32[]{:S(2)}) %collective-permute-start.2) | collective-permute-done | bytes 557088 | tf_op jit(solution)/shard_map/ppermute | solution.py:306
  31.8 2.1 %shard_map.117 = (bf16[8,2048]{1,0:T(8,128)(2,1)S(1)}, bf16[8,2048]{1,0:T(8,128)(2,1)S(1)}, bf16[8,2048]{1,0:T(8,128)(2,1)S(1)}, bf16[8,2048]{1,0:T(8,128)(2,1)S(1)}) custom-call(bf16[3,7,2048]{2,1,0:T(8,128)(2,1)S(1)} %bitcast.16, bf16[288,2048]{1,0:T(8,128)(2,1)S(1)} %bitcast.12, f32[16,2048]{1,0:T(8,128)S(1)} %get-tuple-element.34.first_ref, ...), custom_call_target="tpu_custom_call" | custom-call | flops 1 | bytes 1 | tf_op jit(solution)/shard_map/pallas_call | solution.py:362
  33.9 0.2 collective-permute-start.6
  34.1 2.1 %collective-permute-start.7 = (bf16[8,2048]{1,0:T(8,128)(2,1)S(1)}, bf16[8,2048]{1,0:T(8,128)(2,1)S(1)}, u32[]{:S(2)}, u32[]{:S(2)}) collective-permute-start(bf16[8,2048]{1,0:T(8,128)(2,1)S(1)} %get-tuple-element.38), channel_id=1, source_target_pairs={{0,8},{4,12},{8,0},{12,4},{1,9},{5,13},{9,1},{13,5},{2,10},{6,14},... | collective-permute-start | bytes 98312 | tf_op jit(solution)/shard_map/ppermute | solution.py:306
  36.2 6.6 %shard_map.116 = (f32[12,16,2048]{2,1,0:T(8,128)S(1)}, f32[12,16,2048]{2,1,0:T(8,128)S(1)}) custom-call(s32[1]{0:T(128)} %bitcast.me_ref, s32[12]{0:T(128)S(1)} %copy-done.8, bf16[128,128]{1,0:T(8,128)(2,1)S(1)} %copy-done.4, bf16[3,7,2048]{2,1,0:T(8,128)(2,1)S(1)} %bitcast.17, bf16[12,3,16,2048]{3,2,1,0:T(8,128)(2,1)S(1)} %bitcast.13, ...), custom_call_target="tpu_custom_call" | custom-call | flops 1 | bytes 1 | tf_op jit(solution)/shard_map/pallas_call | solution.py:378
  42.9 0.0 collective-permute-done.4.rest_2_
  42.9 5.2 %collective-permute-done.5.rest_3_ = bf16[6,16,2048]{2,1,0:T(8,128)(2,1)S(1)} collective-permute-done((bf16[6,16,2048]{2,1,0:T(8,128)(2,1)S(1)}, bf16[6,16,2048]{2,1,0:T(8,128)(2,1)S(1)}, u32[]{:S(2)}, u32[]{:S(2)}) %collective-permute-start.5) | collective-permute-done | bytes 393248 | tf_op jit(solution)/shard_map/ppermute | solution.py:306
  48.1 0.0 collective-permute-done.6.rest_5_
  48.1 1.1 %collective-permute-done.7.rest_6_ = bf16[8,2048]{1,0:T(8,128)(2,1)S(1)} collective-permute-done((bf16[8,2048]{1,0:T(8,128)(2,1)S(1)}, bf16[8,2048]{1,0:T(8,128)(2,1)S(1)}, u32[]{:S(2)}, u32[]{:S(2)}) %collective-permute-start.7) | collective-permute-done | bytes 32800 | tf_op jit(solution)/shard_map/ppermute | solution.py:306
  49.2 0.0 collective-permute-done.8.rest_7_
  49.2 1.9 %shard_map.118 = (bf16[12,16,2048]{2,1,0:T(8,128)(2,1)}, bf16[16,2048]{1,0:T(8,128)(2,1)}) custom-call(s32[1]{0:T(128)} %bitcast.me_ref, s32[12]{0:T(128)S(1)} %copy-done.8, s32[16]{0:T(128)S(1)} %copy-done.6, f32[12,16,2048]{2,1,0:T(8,128)S(1)} %get-tuple-element.28.query_ref, f32[12,16,2048]{2,1,0:T(8,128)S(1)} %get-tuple-element.29.conv_ref, ...), custom_call_target="tpu_custom_call" | custom-call | flops 1 | bytes 1 | tf_op jit(solution)/shard_map/pallas_call | solution.py:396
  (18 shorter events, 0.0 us)
Async XLA Ops:
  3.5 17.1 %collective-permute-start.1 = (bf16[136,2048]{1,0:T(8,128)(2,1)}, bf16[136,2048]{1,0:T(8,128)(2,1)S(1)}, u32[]{:S(2)}, u32[]{:S(2)}) collective-permute-start(bf16[136,2048]{1,0:T(8,128)(2,1)} %get-tuple-element.26), channel_id=1, source_target_pairs={{0,8},{4,12},{8,0},{12,4},{1,9},{5,13},{9,1},{13,5},{2,10},{6,14},... | collective-permute-start | bytes 1671176 | tf_op jit(solution)/shard_map/ppermute | solution.py:306
  6.5 25.3 %collective-permute-start.2 = (bf16[136,2048]{1,0:T(8,128)(2,1)}, bf16[136,2048]{1,0:T(8,128)(2,1)S(1)}, u32[]{:S(2)}, u32[]{:S(2)}) collective-permute-start(bf16[136,2048]{1,0:T(8,128)(2,1)} %get-tuple-element.27), channel_id=1, source_target_pairs={{0,12},{4,8},{8,4},{12,0},{1,13},{5,9},{9,5},{13,1},{2,14},{6,10},... | collective-permute-start | bytes 1671176 | tf_op jit(solution)/shard_map/ppermute | solution.py:306
  6.5 0.8 %copy-start.4 = (bf16[128,128]{1,0:T(8,128)(2,1)S(1)}, bf16[128,128]{1,0:T(8,128)(2,1)}, u32[]{:S(2)}) copy-start(bf16[128,128]{1,0:T(8,128)(2,1)} %filter_ref.3) | copy-start | bytes 98308
  7.3 0.7 %copy-start.5 = (s32[1,4,6]{2,1,0:T(4,128)S(1)}, s32[1,4,6]{2,1,0:T(4,128)}, u32[]{:S(2)}) copy-start(s32[1,4,6]{2,1,0:T(4,128)} %slot_hbm.3) | copy-start | bytes 292
  8.0 8.5 %copy-start = (bf16[16,6,3,2048]{3,0,2,1:T(8,128)(2,1)S(1)}, bf16[16,6,3,2048]{3,0,2,1:T(8,128)(2,1)}, u32[]{:S(2)}) copy-start(bf16[16,6,3,2048]{3,0,2,1:T(8,128)(2,1)} %param.16) | copy-start | bytes 3538948
  8.0 8.5 %copy-start.2 = (bf16[16,3,2048]{2,0,1:T(8,128)(2,1)S(1)}, bf16[16,3,2048]{2,0,1:T(8,128)(2,1)}, u32[]{:S(2)}) copy-start(bf16[16,3,2048]{2,0,1:T(8,128)(2,1)} %param.13) | copy-start | bytes 589828
  8.0 8.5 %copy-start.6 = (s32[16]{0:T(128)S(1)}, s32[16]{0:T(128)}, u32[]{:S(2)}) copy-start(s32[16]{0:T(128)} %decode_owner_ref.1) | copy-start | bytes 196
  8.0 8.5 %copy-start.7 = (s32[16]{0:T(128)S(1)}, s32[16]{0:T(128)}, u32[]{:S(2)}) copy-start(s32[16]{0:T(128)} %code_hbm.3) | copy-start | bytes 196
  8.0 23.8 %copy-start.3 = (bf16[7,3,2048]{2,0,1:T(8,128)(2,1)S(1)}, bf16[7,3,2048]{2,0,1:T(8,128)(2,1)}, u32[]{:S(2)}) copy-start(bf16[7,3,2048]{2,0,1:T(8,128)(2,1)} %param.18) | copy-start | bytes 258052
  18.3 13.5 %collective-permute-start = (bf16[136,2048]{1,0:T(8,128)(2,1)S(1)}, bf16[136,2048]{1,0:T(8,128)(2,1)S(1)}, u32[]{:S(2)}, u32[]{:S(2)}) collective-permute-start(bf16[136,2048]{1,0:T(8,128)(2,1)S(1)} %get-tuple-element.25), channel_id=1, source_target_pairs={{0,4},{4,0},{8,12},{12,8},{1,5},{5,1},{9,13},{13,9},{2,6},{6,2},{1... | collective-permute-start | bytes 1671176 | tf_op jit(solution)/shard_map/ppermute | solution.py:306
  18.6 17.6 %collective-permute-start.3 = (bf16[6,16,2048]{2,1,0:T(8,128)(2,1)S(1)}, bf16[6,16,2048]{2,1,0:T(8,128)(2,1)S(1)}, u32[]{:S(2)}, u32[]{:S(2)}) collective-permute-start(bf16[6,16,2048]{2,1,0:T(8,128)(2,1)S(1)} %get-tuple-element.31), channel_id=1, source_target_pairs={{0,4},{4,0},{8,12},{12,8},{1,5},{5,1},{9,13},{13,9},{2,6},{6,2},{1... | collective-permute-start | bytes 1179656 | tf_op jit(solution)/shard_map/ppermute | solution.py:306
  18.9 24.0 %collective-permute-start.4 = (bf16[6,16,2048]{2,1,0:T(8,128)(2,1)S(1)}, bf16[6,16,2048]{2,1,0:T(8,128)(2,1)S(1)}, u32[]{:S(2)}, u32[]{:S(2)}) collective-permute-start(bf16[6,16,2048]{2,1,0:T(8,128)(2,1)S(1)} %get-tuple-element.32), channel_id=1, source_target_pairs={{0,8},{4,12},{8,0},{12,4},{1,9},{5,13},{9,1},{13,5},{2,10},{6,14},... | collective-permute-start | bytes 1179656 | tf_op jit(solution)/shard_map/ppermute | solution.py:306
  20.6 27.5 %collective-permute-start.5 = (bf16[6,16,2048]{2,1,0:T(8,128)(2,1)S(1)}, bf16[6,16,2048]{2,1,0:T(8,128)(2,1)S(1)}, u32[]{:S(2)}, u32[]{:S(2)}) collective-permute-start(bf16[6,16,2048]{2,1,0:T(8,128)(2,1)S(1)} %get-tuple-element.33), channel_id=1, source_target_pairs={{0,12},{4,8},{8,4},{12,0},{1,13},{5,9},{9,5},{13,1},{2,14},{6,10},... | collective-permute-start | bytes 1179656 | tf_op jit(solution)/shard_map/ppermute | solution.py:306
  31.8 4.4 %copy-start.1 = (bf16[12,16,3,2048]{3,1,2,0:T(8,128)(2,1)S(1)}, bf16[12,16,3,2048]{3,1,2,0:T(8,128)(2,1)}, u32[]{:S(2)}) copy-start(bf16[12,16,3,2048]{3,1,2,0:T(8,128)(2,1)} %param.10) | copy-start | bytes 7077892
  31.8 4.4 %copy-start.8 = (s32[12]{0:T(128)S(1)}, s32[12]{0:T(128)}, u32[]{:S(2)}) copy-start(s32[12]{0:T(128)} %owner_ref.3) | copy-start | bytes 148
  33.9 14.2 %collective-permute-start.6 = (bf16[8,2048]{1,0:T(8,128)(2,1)S(1)}, bf16[8,2048]{1,0:T(8,128)(2,1)S(1)}, u32[]{:S(2)}, u32[]{:S(2)}) collective-permute-start(bf16[8,2048]{1,0:T(8,128)(2,1)S(1)} %get-tuple-element.37), channel_id=1, source_target_pairs={{0,4},{4,0},{8,12},{12,8},{1,5},{5,1},{9,13},{13,9},{2,6},{6,2},{1... | collective-permute-start | bytes 98312 | tf_op jit(solution)/shard_map/ppermute | solution.py:306
  34.1 15.0 %collective-permute-start.7 = (bf16[8,2048]{1,0:T(8,128)(2,1)S(1)}, bf16[8,2048]{1,0:T(8,128)(2,1)S(1)}, u32[]{:S(2)}, u32[]{:S(2)}) collective-permute-start(bf16[8,2048]{1,0:T(8,128)(2,1)S(1)} %get-tuple-element.38), channel_id=1, source_target_pairs={{0,8},{4,12},{8,0},{12,4},{1,9},{5,13},{9,1},{13,5},{2,10},{6,14},... | collective-permute-start | bytes 98312 | tf_op jit(solution)/shard_map/ppermute | solution.py:306
  36.2 13.0 %collective-permute-start.8 = (bf16[8,2048]{1,0:T(8,128)(2,1)S(1)}, bf16[8,2048]{1,0:T(8,128)(2,1)S(1)}, u32[]{:S(2)}, u32[]{:S(2)}) collective-permute-start(bf16[8,2048]{1,0:T(8,128)(2,1)S(1)} %get-tuple-element.39), channel_id=1, source_target_pairs={{0,12},{4,8},{8,4},{12,0},{1,13},{5,9},{9,5},{13,1},{2,14},{6,10},... | collective-permute-start | bytes 98312 | tf_op jit(solution)/shard_map/ppermute | solution.py:306
